TPU v7x, 32 devices: a whole 2x2x4 slice. The times are simulated.
32 devices in a mesh: seq: 16 (over z, y, core), head: 2 (over x).
Axes of the slice: x: 2, y: 2, z: 4, core: 2. Of those that a mesh axis runs over, the one named last changes fastest.
Arguments:
- tokens: bfloat16 [16, 1024, 1024], P('seq'), may hold values from -6 to 6
- segment_ids: int32 [16, 1024], P('seq'), may hold values from 0 to 7, as said below
- context_flags: int32 [16, 1024], P('seq'), may hold values from 0 to 1, as said below
- ln1_gain: bfloat16 [1024], replicated, may hold values from 0.25 to 1.75
- ln1_bias: bfloat16 [1024], replicated, may hold values from -4 to 4
- qkv_weight: bfloat16 [3, 1024, 1024], P(None, None, 'head'), may hold values from -0.1875 to 0.1875
- qv_bias: bfloat16 [2, 1024], P(None, 'head'), may hold values from -6 to 6
- out_weight: bfloat16 [1024, 1024], P('head'), may hold values from -1.5 to 1.5
- out_bias: bfloat16 [1024], replicated, may hold values from -4 to 4
- ln2_gain: bfloat16 [1024], replicated, may hold values from 0.25 to 1.75
- ln2_bias: bfloat16 [1024], replicated, may hold values from -4 to 4
- up_weight: bfloat16 [1024, 4096], P('seq', 'head'), may hold values from -0.1875 to 0.1875
- up_bias: bfloat16 [4096], P('head'), may hold values from -6 to 6
- down_weight: bfloat16 [4096, 1024], P('head', 'seq'), may hold values from -0.09375 to 0.09375
- down_bias: bfloat16 [1024], replicated, may hold values from -4 to 4
- cotangent: bfloat16 [16, 1024, 1024], P('seq'), may hold values from -6 to 6
Outputs:
- output: bfloat16 [16, 1024, 1024], P('seq')
- tokens_grad: bfloat16 [16, 1024, 1024], P('seq')
- ln1_gain_grad: float32 [1024], replicated
- ln1_bias_grad: float32 [1024], replicated
- qkv_weight_grad: float32 [3, 1024, 1024], P(None, 'seq', 'head')
- qv_bias_grad: float32 [2, 1024], P(None, 'head')
- out_weight_grad: float32 [1024, 1024], P('head', 'seq')
- out_bias_grad: float32 [1024], replicated
- ln2_gain_grad: float32 [1024], replicated
- ln2_bias_grad: float32 [1024], replicated
- up_weight_grad: float32 [1024, 4096], P('seq', 'head')
- up_bias_grad: float32 [4096], P('head')
- down_weight_grad: float32 [4096, 1024], P('head', 'seq')
- down_bias_grad: float32 [1024], replicated
Inputs may be any that keep to these rules, and one draw needn't show every extreme that they name: `segment_ids`: every sequence holds exactly 8 tables, numbered 0 to 7 in order: the table number starts at 0 at the first row and never falls. `context_flags`: the first row of every table is a context row.
All inputs are finite; a program needn't handle non-finite values.
Results may differ from a plain program's by a relative error of at most 0.015.
Values may be sent and summed in bfloat16 or wider, within the bound.
A program may use at most 192 MiB of HBM per device.

v0:
```python
import math

import jax
import jax.numpy as jnp
from jax import lax
from jax.experimental import pallas as pl
from jax.experimental.pallas import tpu as pltpu
from jax.sharding import PartitionSpec as P

HEAD_DIM = 64


def layer_norm(values_in, scaling, offset):
    middle = jnp.mean(values_in, axis=-1, keepdims=True)
    centred = values_in - middle
    spread = jnp.mean(centred * centred, axis=-1, keepdims=True)
    return centred * lax.rsqrt(spread + 1e-05) * scaling + offset


def gelu_exact(values_in):
    return 0.5 * values_in * (1.0 + jax.scipy.special.erf(values_in * 0.7071067811865476))


def dot_rows(left, right):
    return lax.dot_general(
        left, right, (((1,), (1,)), ((), ())), preferred_element_type=jnp.float32
    )


def dot_cols(left, right):
    return lax.dot_general(
        left, right, (((0,), (0,)), ((), ())), preferred_element_type=jnp.float32
    )


def masked_scores(block_query, seq_keys, block_segments, seq_segments, seq_context, factor):
    raw_scores = (
        jnp.einsum("qhd,khd->hqk", block_query, seq_keys, preferred_element_type=jnp.float32)
        * factor
    )
    allowed = (block_segments[:, None] == seq_segments[None, :]) & (seq_context[None, :] == 1)
    return jnp.where(allowed[None], raw_scores, -1e30)


def generic_body(
    tokens,
    segment_ids,
    context_flags,
    ln1_gain,
    ln1_bias,
    qkv_weight,
    qv_bias,
    out_weight,
    out_bias,
    ln2_gain,
    ln2_bias,
    up_weight,
    up_bias,
    down_weight,
    down_bias,
    cotangent,
):
    seq_count, length, width = tokens.shape
    row_count = seq_count * length
    local_cols = qkv_weight.shape[2]
    head_count = local_cols // HEAD_DIM
    factor = 1.0 / math.sqrt(HEAD_DIM)
    block = min(512, length)
    blocks = length // block
    gain_one = ln1_gain.astype(jnp.float32)
    offset_one = ln1_bias.astype(jnp.float32)
    gain_two = ln2_gain.astype(jnp.float32)
    offset_two = ln2_bias.astype(jnp.float32)
    flat_in = tokens.astype(jnp.float32).reshape(row_count, width)
    normed_f, norm_one_pull = jax.vjp(layer_norm, flat_in, gain_one, offset_one)
    normed = normed_f.astype(jnp.bfloat16)
    queries = (
        jnp.dot(normed, qkv_weight[0], preferred_element_type=jnp.float32)
        + qv_bias[0].astype(jnp.float32)
    ).astype(jnp.bfloat16)
    key_rows = jnp.dot(normed, qkv_weight[1], preferred_element_type=jnp.float32).astype(
        jnp.bfloat16
    )
    value_rows = (
        jnp.dot(normed, qkv_weight[2], preferred_element_type=jnp.float32)
        + qv_bias[1].astype(jnp.float32)
    ).astype(jnp.bfloat16)

    def per_sequence(array):
        return array.reshape(seq_count, length, head_count, HEAD_DIM)

    def attend_sequence(member):
        seq_query, seq_keys, seq_values, seq_segments, seq_context = member

        def attend_block(portion):
            block_query, block_segments = portion
            scores = masked_scores(
                block_query, seq_keys, block_segments, seq_segments, seq_context, factor
            )
            row_top = jnp.max(scores, axis=-1, keepdims=True)
            exponent = jnp.exp(scores - row_top)
            row_total = jnp.sum(exponent, axis=-1, keepdims=True)
            soft_weights = (exponent / row_total).astype(jnp.bfloat16)
            block_mix = jnp.einsum(
                "hqk,khd->qhd", soft_weights, seq_values, preferred_element_type=jnp.float32
            )
            return (block_mix.astype(jnp.bfloat16), row_top + jnp.log(row_total))

        return lax.map(
            attend_block,
            (
                seq_query.reshape(blocks, block, head_count, HEAD_DIM),
                seq_segments.reshape(blocks, block),
            ),
        )

    mixture, log_totals = lax.map(
        attend_sequence,
        (
            per_sequence(queries),
            per_sequence(key_rows),
            per_sequence(value_rows),
            segment_ids,
            context_flags,
        ),
    )
    mixture = mixture.reshape(row_count, local_cols)
    partial_out = jnp.dot(mixture, out_weight, preferred_element_type=jnp.float32)
    grad_rows_all = cotangent.reshape(row_count, width)
    grad_float_all = grad_rows_all.astype(jnp.float32)
    grad_down_bias = jnp.sum(grad_float_all, axis=0)
    attended = lax.psum(partial_out, "head") + out_bias.astype(jnp.float32)
    middle_state = flat_in + attended
    normed_two_f, norm_two_pull = jax.vjp(layer_norm, middle_state, gain_two, offset_two)
    normed_two = normed_two_f.astype(jnp.bfloat16)
    up_part, down_part, up_shift = (
        lax.all_gather(up_weight, "head", axis=1, tiled=True),
        lax.all_gather(down_weight, "head", axis=0, tiled=True),
        lax.all_gather(up_bias, "head", axis=0, tiled=True),
    )
    up_full, down_full = (
        lax.all_gather(up_part, "seq", axis=0, tiled=True),
        lax.all_gather(down_part, "seq", axis=1, tiled=True),
    )
    before = jnp.dot(normed_two, up_full, preferred_element_type=jnp.float32) + up_shift.astype(
        jnp.float32
    )
    active_f, gelu_pull = jax.vjp(gelu_exact, before)
    active = active_f.astype(jnp.bfloat16)
    branch_out = jnp.dot(active, down_full, preferred_element_type=jnp.float32)
    final_rows = (middle_state + branch_out + down_bias.astype(jnp.float32)).astype(jnp.bfloat16)
    output = final_rows.reshape(tokens.shape)
    grad_float = grad_rows_all.astype(jnp.float32)
    grad_down = dot_cols(active, grad_rows_all)
    grad_active = dot_rows(grad_rows_all, down_full)
    (grad_before_f,) = gelu_pull(grad_active)
    grad_before = grad_before_f.astype(jnp.bfloat16)
    grad_up = dot_cols(normed_two, grad_before)
    grad_up_bias = jnp.sum(grad_before.astype(jnp.float32), axis=0)
    grad_normed_two = dot_rows(grad_before, up_full)
    grad_middle_norm, grad_gain_two, grad_offset_two = norm_two_pull(grad_normed_two)
    grad_middle = grad_float + grad_middle_norm
    ff_part = up_weight.shape[1]
    start_col = lax.axis_index("head") * ff_part
    grad_up = lax.dynamic_slice_in_dim(grad_up, start_col, ff_part, 1)
    grad_down = lax.dynamic_slice_in_dim(grad_down, start_col, ff_part, 0)
    grad_up_bias = lax.dynamic_slice_in_dim(grad_up_bias, start_col, ff_part, 0)
    grad_attended = grad_middle.astype(jnp.bfloat16)
    grad_out_bias = jnp.sum(grad_attended.astype(jnp.float32), axis=0)
    grad_out = dot_cols(mixture, grad_attended)
    grad_mixture = dot_rows(grad_attended, out_weight).astype(jnp.bfloat16)

    def back_sequence(member):
        seq_query, seq_keys, seq_values, seq_grad, seq_logs, seq_segments, seq_context = member

        def back_block(carry, portion):
            key_acc, value_acc = carry
            block_query, block_grad, block_logs, block_segments = portion
            scores = masked_scores(
                block_query, seq_keys, block_segments, seq_segments, seq_context, factor
            )
            soft_weights = jnp.exp(scores - block_logs)
            value_acc = value_acc + jnp.einsum(
                "hqk,qhd->khd",
                soft_weights.astype(jnp.bfloat16),
                block_grad,
                preferred_element_type=jnp.float32,
            )
            grad_soft = jnp.einsum(
                "qhd,khd->hqk", block_grad, seq_values, preferred_element_type=jnp.float32
            )
            row_inner = jnp.sum(soft_weights * grad_soft, axis=-1, keepdims=True)
            grad_scores = (soft_weights * (grad_soft - row_inner)).astype(jnp.bfloat16)
            grad_query = (
                jnp.einsum(
                    "hqk,khd->qhd", grad_scores, seq_keys, preferred_element_type=jnp.float32
                )
                * factor
            )
            key_acc = (
                key_acc
                + jnp.einsum(
                    "hqk,qhd->khd", grad_scores, block_query, preferred_element_type=jnp.float32
                )
                * factor
            )
            return ((key_acc, value_acc), grad_query)

        empty = jnp.zeros((length, head_count, HEAD_DIM), jnp.float32)
        (key_acc, value_acc), grad_query = lax.scan(
            back_block,
            (empty, empty),
            (
                seq_query.reshape(blocks, block, head_count, HEAD_DIM),
                seq_grad.reshape(blocks, block, head_count, HEAD_DIM),
                seq_logs,
                seq_segments.reshape(blocks, block),
            ),
        )
        return (grad_query, key_acc, value_acc)

    grad_queries, grad_keys, grad_values = lax.map(
        back_sequence,
        (
            per_sequence(queries),
            per_sequence(key_rows),
            per_sequence(value_rows),
            per_sequence(grad_mixture),
            log_totals,
            segment_ids,
            context_flags,
        ),
    )
    grad_queries = grad_queries.reshape(row_count, local_cols).astype(jnp.bfloat16)
    grad_keys = grad_keys.reshape(row_count, local_cols).astype(jnp.bfloat16)
    grad_values = grad_values.reshape(row_count, local_cols).astype(jnp.bfloat16)
    grad_qv_bias = jnp.stack(
        [
            jnp.sum(grad_queries.astype(jnp.float32), axis=0),
            jnp.sum(grad_values.astype(jnp.float32), axis=0),
        ]
    )
    grad_qkv = jnp.stack(
        [dot_cols(normed, grad_queries), dot_cols(normed, grad_keys), dot_cols(normed, grad_values)]
    )
    grad_normed = (
        dot_rows(grad_queries, qkv_weight[0])
        + dot_rows(grad_keys, qkv_weight[1])
        + dot_rows(grad_values, qkv_weight[2])
    )
    grad_normed = lax.psum(grad_normed, "head")
    grad_input_norm, grad_gain_one, grad_offset_one = norm_one_pull(grad_normed)
    tokens_grad = (grad_middle + grad_input_norm).astype(jnp.bfloat16).reshape(tokens.shape)
    summed_qkv, summed_out, summed_up, summed_down = (
        lax.psum_scatter(
            grad_qkv.astype(jnp.bfloat16), "seq", scatter_dimension=1, tiled=True
        ).astype(jnp.float32),
        lax.psum_scatter(
            grad_out.astype(jnp.bfloat16), "seq", scatter_dimension=1, tiled=True
        ).astype(jnp.float32),
        lax.psum_scatter(
            grad_up.astype(jnp.bfloat16), "seq", scatter_dimension=0, tiled=True
        ).astype(jnp.float32),
        lax.psum_scatter(
            grad_down.astype(jnp.bfloat16), "seq", scatter_dimension=1, tiled=True
        ).astype(jnp.float32),
    )
    smalls = lax.psum(
        (
            grad_gain_one,
            grad_offset_one,
            grad_qv_bias,
            grad_out_bias,
            grad_gain_two,
            grad_offset_two,
            grad_up_bias,
            grad_down_bias,
        ),
        "seq",
    )
    return (
        output,
        tokens_grad,
        smalls[0],
        smalls[1],
        summed_qkv,
        smalls[2],
        summed_out,
        smalls[3],
        smalls[4],
        smalls[5],
        summed_up,
        smalls[6],
        summed_down,
        smalls[7],
    )


MESH = pl.DeviceIdType.MESH
BF = jnp.bfloat16
F32 = jnp.float32
BLOCK = 256
STRIP = 512
PIECE = 128
WIDE = 1024
GROUP = 2
CHUNK = 512
PAIR = 2 * HEAD_DIM
Z_SIZE, Y_SIZE, CORES = 4, 2, 2
SEQ_SIZE = Z_SIZE * Y_SIZE * CORES
HOP = Y_SIZE * CORES
TABLES = 8
FAR = -1e30
VMEM_LIMIT = 62 * 2**20
INV_ROOT_TWO = 0.7071067811865476
INV_ROOT_TWO_PI = 0.3989422804014327
LN1_GAIN, LN1_BIAS, QV_BIAS, OUT_BIAS, LN2_GAIN, LN2_BIAS, UP_BIAS, DOWN_BIAS = 0, 1, 2, 3, 4, 5, 6, 8
SMALL_ROWS = 16
VMEM_SPEC = pl.BlockSpec(memory_space=pltpu.VMEM)
ANY_SPEC = pl.BlockSpec(memory_space=pl.ANY)


def shape_of(dims, dtype):
    return jax.ShapeDtypeStruct(tuple(dims), dtype)


def nn(left, right):
    return jnp.dot(left, right, preferred_element_type=F32)


def split_sum(left, right):
    parts = [
        nn(left[:, n:n + BLOCK], right[n:n + BLOCK]) for n in range(0, left.shape[1], BLOCK)
    ]
    while len(parts) > 1:
        parts = [a + b for a, b in zip(parts[::2], parts[1::2])]
    return parts[0]


def turn(block):
    return jnp.transpose(block)


def sum_rows(block):
    return jnp.sum(block, axis=0, keepdims=True)


def place():
    me = lax.axis_index("seq")
    head = lax.axis_index("head")
    core = me % 2
    y = (me // 2) % 2
    across = {"seq": me, "head": 1 - head}
    core_mate = {"seq": me + 1 - 2 * core, "head": head}
    y_mate = {"seq": me + 2 - 4 * y, "head": head}
    z_mates = [{"seq": (me + HOP * d) % SEQ_SIZE, "head": head} for d in (1, 2, 3)]
    return me, head, core, y, across, core_mate, y_mate, z_mates


def greet(others):
    barrier = pltpu.get_barrier_semaphore()
    for other in others:
        pl.semaphore_signal(barrier, inc=1, device_id=other, device_id_type=MESH)
    pl.semaphore_wait(barrier, len(others))


def remote(src, dst, send_sem, recv_sem, other):
    return pltpu.make_async_remote_copy(
        src_ref=src, dst_ref=dst, send_sem=send_sem, recv_sem=recv_sem,
        device_id=other, device_id_type=MESH,
    )


def norm_stats(rows):
    middle = jnp.mean(rows, axis=-1, keepdims=True)
    centred = rows - middle
    spread = jnp.mean(centred * centred, axis=-1, keepdims=True)
    return centred, lax.rsqrt(spread + 1e-05)


def norm_back(inner, unit, scale):
    return scale * (
        inner
        - jnp.mean(inner, axis=-1, keepdims=True)
        - unit * jnp.mean(inner * unit, axis=-1, keepdims=True)
    )


def as_row(vector):
    return vector[...].astype(F32).reshape(1, -1)


def lanes():
    return lax.broadcasted_iota(jnp.int32, (1, PAIR), 1)


def in_pieces(column, first, rest):
    high = column.astype(BF).astype(F32)
    mid = (column - high).astype(BF).astype(F32)
    low = column - high - mid
    at = lanes()
    return jnp.where(
        at == first, high, jnp.where(at == first + 1, mid, jnp.where(at == first + 2, low, rest))
    ).astype(BF)


def one_lanes(length):
    return jnp.broadcast_to(jnp.where(lanes() < 3, 1.0, 0.0).astype(BF), (length, PAIR))


def fwd_kernel(
    x_ref, seg_ref, context, gain, offset, qv_bias, out_bias, gain_two, offset_two, up_bias,
    wqkv, wout, up_shard, down_shard,
    q_out, k_out, v_out, mix_out, mid_out, normed_out, wff_out, key_out, query_out,
    normed_two_out, active_out, slope_out,
    wff, q_ref, k_ref, v_ref, mix_ref, mid_ref, normed_t, key_more, query_more,
    normed_two_t, active, slope, bias_row, mask_more, wout_x, mix_x,
    zs, zr, ys, yr, cs, cr, xs, xr, local, outs,
):
    length, width = x_ref.shape
    blocks = length // BLOCK
    pairs = q_ref.shape[0]
    cols = pairs * PAIR
    me, head, core, y, across, core_mate, y_mate, _ = place()
    z = me // HOP
    above = {"seq": (me + HOP) % SEQ_SIZE, "head": head}
    below = {"seq": (me + SEQ_SIZE - HOP) % SEQ_SIZE, "head": head}
    own = [
        pltpu.make_async_copy(shard, wff.at[u, me], local.at[u])
        for u, shard in enumerate((up_shard, down_shard))
    ]
    own[0].start()
    own[1].start()
    greet([across, core_mate, y_mate, above, below])

    half = wout.shape[0] // 2
    here = pl.ds(pl.multiple_of(core * half, half), half)
    beside = pl.ds(pl.multiple_of((1 - core) * half, half), half)
    out_copy = remote(wout.at[here, :], wout_x.at[here, :], xs.at[0], xr.at[0], across)
    out_pass = remote(wout_x.at[here, :], wout_x.at[here, :], cs.at[28], cr.at[28], core_mate)
    out_arrival = remote(
        wout_x.at[beside, :], wout_x.at[beside, :], cs.at[28], cr.at[28], core_mate
    )
    out_copy.start()

    flows = [(0, 0)] + [(way, s) for s in (1, 2, 3) for way in (0, 1)]

    def there(way, s):
        return (z >= s) if way == 0 else (z + s < Z_SIZE)

    def source(base, way, s):
        away = SEQ_SIZE - HOP * s if way == 0 else HOP * s
        return (base + away) % SEQ_SIZE

    def z_copy(u, way, s):
        n = (u * 2 + way) * 3 + s - 1
        j = source(me, way, s - 1)
        return remote(wff.at[u, j], wff.at[u, j], zs.at[n], zr.at[n], above if way == 0 else below)

    def z_arrival(u, way, s):
        n = (u * 2 + way) * 3 + s - 1
        slot = wff.at[u, source(me, way, s)]
        return remote(slot, slot, zs.at[n], zr.at[n], above)

    def z_goes_on(way):
        return (z < Z_SIZE - 1) if way == 0 else (z > 0)

    def y_copy(u, f):
        n = u * 7 + f
        j = source(me, *flows[f])
        return remote(wff.at[u, j], wff.at[u, j], ys.at[n], yr.at[n], y_mate)

    def y_arrival(u, f):
        n = u * 7 + f
        slot = wff.at[u, source(me + 2 - 4 * y, *flows[f])]
        return remote(slot, slot, ys.at[n], yr.at[n], y_mate)

    def c_copy(u, f, from_y):
        n = (u * 2 + from_y) * 7 + f
        j = source(me + from_y * (2 - 4 * y), *flows[f])
        return remote(wff.at[u, j], wff.at[u, j], cs.at[n], cr.at[n], core_mate)

    def c_arrival(u, f, from_y):
        n = (u * 2 + from_y) * 7 + f
        slot = wff.at[u, source(me + 1 - 2 * core + from_y * (2 - 4 * y), *flows[f])]
        return remote(slot, slot, cs.at[n], cr.at[n], core_mate)

    def for_flow(f, do):
        if f == 0:
            do()
        else:
            pl.when(there(*flows[f]))(do)

    def for_step(s, do):
        for f, (way, step) in enumerate(flows):
            if step == s:
                for_flow(f, lambda f=f, way=way: do(f, way))

    def z_event(u, s):
        def one(f, way):
            z_arrival(u, way, s).wait_recv()
            if s < 3:
                pl.when(z_goes_on(way))(lambda: z_copy(u, way, s + 1).start())
            y_copy(u, f).start()
            c_copy(u, f, 0).start()
        for_step(s, one)
        if u == 0 and s == 1:
            start_z(1)
        if u == 0 and s == 2:
            y_copy(1, 0).start()
            c_copy(1, 0, 0).start()
        if u == 0 and s == 3:
            out_copy.wait_recv()
            out_pass.start()

    def y_event(u, s):
        def one(f, way):
            y_arrival(u, f).wait_recv()
            c_copy(u, f, 1).start()
        for_step(s, one)

    def start_z(u):
        for way in (0, 1):
            pl.when(z_goes_on(way))(lambda way=way: z_copy(u, way, 1).start())

    own[0].wait()
    start_z(0)
    y_copy(0, 0).start()
    c_copy(0, 0, 0).start()
    own[1].wait()

    plan = {
        2: [(z_event, 0, 1), (y_event, 0, 0)], 4: [(z_event, 0, 2)], 5: [(y_event, 0, 1)],
        6: [(z_event, 0, 3)], 7: [(z_event, 1, 1)], 8: [(y_event, 0, 2), (y_event, 1, 0)],
        9: [(z_event, 1, 2)], 10: [(y_event, 0, 3)], 11: [(z_event, 1, 3)],
    }

    def tick(t):
        for step, events in plan.items():
            @pl.when(t == step)
            def _(events=events):
                for event, u, s in events:
                    event(u, s)

    at = lax.broadcasted_iota(jnp.int32, (PAIR, length), 0)
    same = at == seg_ref[...]
    hidden = context[...] != 1
    ones = jnp.logical_and(at > TABLES, at < TABLES + 4)
    key_side = jnp.logical_or(
        jnp.logical_and(at < TABLES, same),
        jnp.logical_or(jnp.logical_and(at == TABLES, hidden), ones),
    )
    query_side = jnp.logical_and(at <= TABLES, jnp.logical_not(same))
    key_more[...] = turn(jnp.where(key_side, 1.0, 0.0)).astype(BF)
    mask_more[...] = turn(jnp.where(query_side, FAR, 0.0)).astype(BF)

    keep = [
        pltpu.make_async_copy(here, there, outs.at[n])
        for n, (here, there) in enumerate(
            (
                (q_ref, q_out), (k_ref, k_out), (v_ref, v_out), (normed_t, normed_out),
                (key_more, key_out), (query_more, query_out), (mix_ref, mix_out),
            )
        )
    ]
    gains, offsets = as_row(gain), as_row(offset)
    query_bias = qv_bias[0:1, :].astype(F32)
    value_bias = qv_bias[1:2, :].astype(F32)

    def project(b, _):
        rows = pl.ds(pl.multiple_of(b * BLOCK, BLOCK), BLOCK)
        centred, scale = norm_stats(x_ref[rows, :].astype(F32))
        block = (centred * scale * gains + offsets).astype(BF)
        normed_t[:, rows] = turn(block)
        queries = ((nn(block, wqkv[0]) + query_bias).astype(BF) * 0.125).astype(BF)
        keys = nn(block, wqkv[1]).astype(BF)
        values = (nn(block, wqkv[2]) + value_bias).astype(BF)
        for p in range(pairs):
            part = slice(p * PAIR, (p + 1) * PAIR)
            q_ref[p, rows, :] = queries[:, part]
            k_ref[p, rows, :] = keys[:, part]
            v_ref[p, rows, :] = values[:, part]
        tick(b)
        return 0

    lax.fori_loop(0, blocks, project, 0)
    for n in range(5):
        keep[n].start()

    low_lanes = lanes() < HEAD_DIM
    zero = jnp.zeros((1, PAIR), BF)

    def mixture_copy(t):
        rows = pl.ds(pl.multiple_of(t // pairs * STRIP, STRIP), STRIP)
        return remote(
            mix_ref.at[t % pairs, rows, :], mix_x.at[t % pairs, rows, :], xs.at[1 + t],
            xr.at[1 + t], across,
        )

    per_step = STRIP // BLOCK

    def attend(t, _):
        b, p = t // pairs, t % pairs
        keys = jnp.concatenate([k_ref[p], key_more[...]], axis=1)
        values = jnp.concatenate([v_ref[p], one_lanes(length)], axis=1)
        chains = []
        for n in range(per_step):
            rows = pl.ds(pl.multiple_of(b * STRIP + n * BLOCK, BLOCK), BLOCK)
            queries, more = q_ref[p, rows, :], mask_more[rows, :]
            for low in (0, 1):
                own_lanes = jnp.logical_not(low_lanes) if low else low_lanes
                left = jnp.concatenate([jnp.where(own_lanes, queries, zero), more], axis=1)
                chains.append((rows, low, more, dot_rows(left, keys)))
        parts = []
        for rows, low, more, scores in chains:
            top = jnp.max(scores, axis=-1, keepdims=True)
            mixed = nn(jnp.exp(scores - top).astype(BF), values)
            total = mixed[:, PAIR:PAIR + 1]
            parts.append(mixed[:, :PAIR] / total)
            query_more[2 * p + low, rows, :] = in_pieces(
                -(top + jnp.log(total)), TABLES + 1, more.astype(F32)
            )
            if low:
                mix_ref[p, rows, :] = jnp.where(low_lanes, *parts[-2:]).astype(BF)
        mixture_copy(t).start()
        tick(t + blocks)
        return 0

    lax.fori_loop(0, length // STRIP * pairs, attend, 0)
    keep[5].start()
    keep[6].start()
    out_arrival.wait_recv()
    out_row = as_row(out_bias)

    def mid_copy(b):
        rows = pl.ds(b * BLOCK, BLOCK)
        return pltpu.make_async_copy(mid_ref.at[rows, :], mid_out.at[rows, :], outs.at[7 + b])

    gains_two, offsets_two = as_row(gain_two), as_row(offset_two)
    bias_row[...] = as_row(up_bias)

    def half_copies(b):
        rows = pl.ds(b * BLOCK, BLOCK)
        return [
            pltpu.make_async_copy(
                here.at[:, rows, :], there.at[:, rows, :], outs.at[7 + blocks + 2 * b + n]
            )
            for n, (here, there) in enumerate(((active, active_out), (slope, slope_out)))
        ]

    def up_half(b):
        rows = pl.ds(b * BLOCK, BLOCK)
        centred, scale = norm_stats(mid_ref[rows, :])
        block = (centred * scale * gains_two + offsets_two).astype(BF)
        normed_two_t[:, rows] = turn(block)

        def one(n, _):
            cut = pl.ds(pl.multiple_of(n * WIDE, WIDE), WIDE)
            before = nn(block, wff[0, :, :, cut].reshape(width, WIDE)) + bias_row[:, cut]
            spread = 0.5 * (1.0 + lax.erf(before * INV_ROOT_TWO))
            active[n, rows, :] = (before * spread).astype(BF)
            bell = INV_ROOT_TWO_PI * jnp.exp(before * before * -0.5)
            slope[n, rows, :] = (spread + before * bell).astype(BF)
            return 0

        lax.fori_loop(0, active.shape[0], one, 0)
        for copy in half_copies(b):
            copy.start()

    def arrive(u):
        for f in range(len(flows)):
            def one(f=f):
                for from_y in (0, 1):
                    c_arrival(u, f, from_y).wait_recv()
            for_flow(f, one)

    for b in range(blocks):
        if b % per_step == 0:
            for p in range(pairs):
                mixture_copy(b // per_step * pairs + p).wait_recv()
        rows = pl.ds(b * BLOCK, BLOCK)
        ours = jnp.concatenate([mix_ref[p, rows, :] for p in range(pairs)], axis=-1)
        other = jnp.concatenate([mix_x[p, rows, :] for p in range(pairs)], axis=-1)
        attended = nn(ours, wout[...]) + nn(other, wout_x[...])
        mid_ref[rows, :] = x_ref[rows, :].astype(F32) + (attended + out_row)
        mid_copy(b).start()
        if b == 0:
            arrive(0)
        up_half(b)
        if b < 3:
            y_event(1, b + 1)
    normed_two_keep = pltpu.make_async_copy(
        normed_two_t, normed_two_out, outs.at[7 + 3 * blocks]
    )
    normed_two_keep.start()
    wff_keep = [pltpu.make_async_copy(wff.at[u], wff_out.at[u], local.at[u]) for u in range(2)]
    wff_keep[0].start()
    arrive(1)
    wff_keep[1].start()
    out_copy.wait_send()
    out_pass.wait_send()
    for copy in keep + wff_keep + [normed_two_keep]:
        copy.wait()
    for b in range(blocks):
        for copy in half_copies(b):
            copy.wait()
    for t in range(length // STRIP * pairs):
        mixture_copy(t).wait_send()
    for b in range(blocks):
        mid_copy(b).wait()
    for u in range(2):
        for way in (0, 1):
            pl.when(z_goes_on(way))(lambda u=u, way=way: z_copy(u, way, 1).wait_send())
        for f, (way, s) in enumerate(flows):
            def finish(u=u, f=f, way=way, s=s):
                if f and s < 3:
                    pl.when(z_goes_on(way))(lambda: z_copy(u, way, s + 1).wait_send())
                y_copy(u, f).wait_send()
                for from_y in (0, 1):
                    c_copy(u, f, from_y).wait_send()
            for_flow(f, finish)


def run_fwd(
    x, seg, context, gain, offset, qv_bias, out_bias, gain_two, offset_two, up_bias, wqkv, wout,
    up_weight, down_t,
):
    length, width = x.shape
    pairs = wqkv.shape[2] // PAIR
    blocks = length // BLOCK
    depth, hidden = up_weight.shape
    by_pair, by_head = (pairs, length, PAIR), (2 * pairs, length, PAIR)
    turned = (width, length)
    halves = (hidden // WIDE, length, WIDE)
    steps = length // STRIP * pairs
    dma = pltpu.SemaphoreType.DMA
    return pl.pallas_call(
        fwd_kernel,
        out_shape=[shape_of(by_pair, BF)] * 4 + [
            shape_of((length, width), F32),
            shape_of(turned, BF),
            shape_of((2, SEQ_SIZE, depth, hidden), BF),
            shape_of((length, PAIR), BF),
            shape_of(by_head, BF),
            shape_of((width, length), BF),
            shape_of(halves, BF),
            shape_of(halves, BF),
        ],
        in_specs=[VMEM_SPEC] * 12 + [ANY_SPEC] * 2,
        out_specs=[ANY_SPEC] * 12,
        scratch_shapes=[pltpu.VMEM((2, SEQ_SIZE, depth, hidden), BF)]
        + [pltpu.VMEM(by_pair, BF)] * 4 + [
            pltpu.VMEM((length, width), F32),
            pltpu.VMEM(turned, BF),
            pltpu.VMEM((length, PAIR), BF),
            pltpu.VMEM(by_head, BF),
            pltpu.VMEM((width, length), BF),
            pltpu.VMEM(halves, BF),
            pltpu.VMEM(halves, BF),
            pltpu.VMEM((1, hidden), F32),
            pltpu.VMEM((length, PAIR), BF),
            pltpu.VMEM(wout.shape, BF),
            pltpu.VMEM(by_pair, BF),
            dma((12,)), dma((12,)), dma((14,)), dma((14,)), dma((29,)), dma((29,)),
            dma((1 + steps,)), dma((1 + steps,)), dma((2,)), dma((8 + 3 * blocks,)),
        ],
        compiler_params=pltpu.CompilerParams(
            collective_id=0, has_side_effects=True, vmem_limit_bytes=VMEM_LIMIT
        ),
    )(
        x, seg, context, gain, offset, qv_bias, out_bias, gain_two, offset_two, up_bias, wqkv,
        wout, up_weight, down_t,
    )


def ff_kernel(
    mid_hbm, dy_hbm, wff_hbm, normed_two_hbm, active_hbm, slope_hbm, gain, wout_hbm,
    branch_out, gmid_hbm, ga_out, gm_out, summed, small_ref,
    dy_ref, wff, wout, branch_ref, ga_t, gm_ref, normed_t, dy_t, active, before_grad, gnt_acc, gnt_own, gnt_x, whole, from_mate,
    held, ready,
    xs, xr, cs, cr, ls, ws, ss, ins, outs,
):
    length, width = dy_ref.shape
    blocks = length // BLOCK
    hidden = wff.shape[3]
    half = hidden // WIDE
    chunks = 2 * hidden // CHUNK
    pairs = gm_ref.shape[0]
    me, head, core, y, across, core_mate, y_mate, z_mates = place()
    dy_load = pltpu.make_async_copy(dy_hbm, dy_ref, ins.at[0])
    wout_load = pltpu.make_async_copy(wout_hbm, wout, ins.at[1])

    def step_loads(n):
        cut = pl.ds(n * WIDE, WIDE)
        return [
            pltpu.make_async_copy(src, dst, ins.at[4 + 3 * n + m])
            for m, (src, dst) in enumerate(
                (
                    (wff_hbm.at[1, :, :, cut], wff.at[1, :, :, cut]),
                    (slope_hbm.at[n], before_grad.at[n]),
                    (wff_hbm.at[0, :, :, cut], wff.at[0, :, :, cut]),
                )
            )
        ]

    active_load = pltpu.make_async_copy(active_hbm, active, ins.at[2])
    normed_load = pltpu.make_async_copy(normed_two_hbm, normed_t, ins.at[3])
    dy_load.start()
    for n in range(half):
        for copy in step_loads(n):
            copy.start()
    active_load.start()
    normed_load.start()
    wout_load.start()
    greet([across, core_mate])
    gains = as_row(gain)

    def weight(kind, n):
        cut = pl.ds(pl.multiple_of(n * WIDE, WIDE), WIDE)
        return wff[kind, :, :, cut].reshape(width, WIDE)

    small_ref[...] = jnp.zeros_like(small_ref)

    def load(b):
        rows = pl.ds(b * BLOCK, BLOCK)
        return pltpu.make_async_copy(mid_hbm.at[rows, :], held.at[b % 2], ls.at[b % 2])

    def store(b):
        rows = pl.ds(b * BLOCK, BLOCK)
        return pltpu.make_async_copy(ready.at[b % 2], gmid_hbm.at[rows, :], ws.at[b % 2])

    load(0).start()
    load(1).start()

    def gnt_copy(b):
        return remote(gnt_own.at[b], gnt_x.at[b], xs.at[b], xr.at[b], across)

    def core_copy(n):
        return remote(
            whole.at[n, :, :, 1 - core], from_mate.at[n], cs.at[n], cr.at[n], core_mate
        )

    def forward(t, _):
        b, n = t // half, t % half
        rows = pl.ds(pl.multiple_of(b * BLOCK, BLOCK), BLOCK)

        for n_first in range(half):
            @pl.when(t == n_first)
            def _(n_first=n_first):
                if n_first == 0:
                    dy_load.wait()
                for copy in step_loads(n_first):
                    copy.wait()

        @pl.when(n == 0)
        def _():
            dy_t[:, rows] = turn(dy_ref[rows, :])
            small_ref[DOWN_BIAS:DOWN_BIAS + 1, :] += sum_rows(dy_ref[rows, :].astype(F32))

        up = weight(0, n)
        grad = nn(dy_ref[rows, :], weight(1, n)) * before_grad[n, rows, :].astype(F32)
        grad = grad.astype(BF)
        before_grad[n, rows, :] = grad
        small_ref[pl.ds(UP_BIAS + n, 1), :] += sum_rows(grad.astype(F32))
        back = dot_rows(grad, up)

        @pl.when(n == 0)
        def _():
            gnt_acc[...] = back

        @pl.when(n > 0)
        def _():
            gnt_acc[...] += back

        for b_done in range(blocks):
            @pl.when(t == (b_done + 1) * half - 1)
            def _(b_done=b_done):
                gnt_own[b_done] = gnt_acc[...].astype(BF)
                gnt_copy(b_done).start()
        return 0

    lax.fori_loop(0, blocks * half, forward, 0)

    def weight_grads(left_t, right, first):
        cut_rows = width // Z_SIZE
        per_wide = WIDE // CHUNK

        def one(t, _):
            n, plane = t // Z_SIZE, t % Z_SIZE
            cut = pl.ds(pl.multiple_of(plane * cut_rows, cut_rows), cut_rows)
            total = nn(left_t[cut, :], right[n]).astype(BF)
            for m in range(per_wide):
                piece = total[:, m * CHUNK:(m + 1) * CHUNK]
                whole[first + n * per_wide + m, plane] = piece.reshape(whole.shape[2:])

            @pl.when(plane == Z_SIZE - 1)
            def _():
                for m in range(per_wide):
                    core_copy(first + n * per_wide + m).start()

            return 0

        lax.fori_loop(0, Z_SIZE * half, one, 0)

    active_load.wait()
    normed_load.wait()
    weight_grads(dy_t, active, chunks // 2)
    weight_grads(normed_t, before_grad, 0)

    def branch(b, _):
        rows = pl.ds(pl.multiple_of(b * BLOCK, BLOCK), BLOCK)
        total = dot_rows(active[0, rows, :], weight(1, 0))
        for n in range(1, half):
            total += dot_rows(active[n, rows, :], weight(1, n))
        branch_ref[rows, :] = total.astype(BF)
        return 0

    lax.fori_loop(0, blocks, branch, 0)
    branch_keep = pltpu.make_async_copy(branch_ref, branch_out, outs.at[0])
    branch_keep.start()
    wout_load.wait()

    def ga_copy(b):
        rows = pl.ds(b * BLOCK, BLOCK)
        return pltpu.make_async_copy(ga_t.at[:, rows], ga_out.at[:, rows], outs.at[1 + b])

    def gm_copy(b):
        rows = pl.ds(b * BLOCK, BLOCK)
        return pltpu.make_async_copy(
            gm_ref.at[:, rows, :], gm_out.at[:, rows, :], outs.at[1 + blocks + b]
        )


    def add_mate(n, _):
        core_copy(n).wait()
        both = whole[n, :, :, core].astype(F32) + from_mate[n].astype(F32)
        from_mate[n] = both.astype(BF)
        return 0

    lax.fori_loop(chunks // 2, chunks, add_mate, 0)
    lax.fori_loop(0, chunks // 2, add_mate, 0)
    keep = pltpu.make_async_copy(from_mate, summed, ss.at[0])
    keep.start()

    strips = BLOCK // PIECE
    for b in range(blocks):
        gnt_copy(b).wait()
        load(b).wait()
        if b >= 2:
            store(b - 2).wait()

        def through_norm(n, _, b=b):
            rows = pl.ds(pl.multiple_of(n * PIECE, PIECE), PIECE)
            full = pl.ds(pl.multiple_of(b * BLOCK + n * PIECE, PIECE), PIECE)
            grad = gnt_own[b, rows, :].astype(F32) + gnt_x[b, rows, :].astype(F32)
            centred, scale = norm_stats(held[b % 2, rows, :])
            unit = centred * scale
            small_ref[LN2_GAIN:LN2_GAIN + 1, :] += sum_rows(grad * unit)
            small_ref[LN2_BIAS:LN2_BIAS + 1, :] += sum_rows(grad)
            total = dy_ref[full, :].astype(F32) + norm_back(grad * gains, unit, scale)
            ready[b % 2, rows, :] = total
            low = total.astype(BF)
            small_ref[OUT_BIAS:OUT_BIAS + 1, :] += sum_rows(low.astype(F32))
            ga_t[:, full] = turn(low)
            mixed = dot_rows(low, wout[...]).astype(BF)
            for p in range(pairs):
                gm_ref[p, full, :] = mixed[:, p * PAIR:(p + 1) * PAIR]
            return 0

        lax.fori_loop(0, strips, through_norm, 0)
        store(b).start()
        ga_copy(b).start()
        gm_copy(b).start()
        if b + 2 < blocks:
            load(b + 2).start()
    store(blocks - 2).wait()
    store(blocks - 1).wait()
    for b in range(blocks):
        ga_copy(b).wait()
        gm_copy(b).wait()
    branch_keep.wait()
    keep.wait()


def run_ff(middle, dy, wff, normed_two_t, active, slope, gain, wout):
    length, width = middle.shape
    half = wff.shape[3] // WIDE
    chunks = 2 * wff.shape[3] // CHUNK
    blocks = length // BLOCK
    pairs = wout.shape[0] // PAIR
    depth = width // SEQ_SIZE
    dma = pltpu.SemaphoreType.DMA
    rows = pltpu.VMEM((blocks, BLOCK, width), BF)
    hidden = pltpu.VMEM((half, length, WIDE), BF)
    flat_t = pltpu.VMEM((width, length), BF)
    return pl.pallas_call(
        ff_kernel,
        out_shape=[
            shape_of((length, width), BF),
            shape_of((length, width), F32),
            shape_of((width, length), BF),
            shape_of((pairs, length, PAIR), BF),
            shape_of((chunks, Z_SIZE, Y_SIZE, depth, CHUNK), BF),
            shape_of((SMALL_ROWS, width), F32),
        ],
        in_specs=[ANY_SPEC] * 6 + [VMEM_SPEC, ANY_SPEC],
        out_specs=[ANY_SPEC] * 5 + [VMEM_SPEC],
        scratch_shapes=[
            pltpu.VMEM((length, width), BF), pltpu.VMEM(wff.shape, BF),
            pltpu.VMEM(wout.shape, BF),
            pltpu.VMEM((length, width), BF), flat_t, pltpu.VMEM((pairs, length, PAIR), BF),
            flat_t, flat_t, hidden, hidden,
            pltpu.VMEM((BLOCK, width), F32), rows, rows,
            pltpu.VMEM((chunks, Z_SIZE, Y_SIZE, CORES, depth, CHUNK), BF),
            pltpu.VMEM((chunks, Z_SIZE, Y_SIZE, depth, CHUNK), BF),
            pltpu.VMEM((2, BLOCK, width), F32), pltpu.VMEM((2, BLOCK, width), F32),
            dma((blocks,)), dma((blocks,)), dma((chunks,)), dma((chunks,)),
            dma((2,)), dma((2,)), dma((1,)), dma((4 + 3 * half,)), dma((1 + 2 * blocks,)),
        ],
        compiler_params=pltpu.CompilerParams(
            collective_id=1, has_side_effects=True, vmem_limit_bytes=VMEM_LIMIT
        ),
    )(middle, dy, wff, normed_two_t, active, slope, gain, wout)


def back_kernel(
    q_hbm, k_hbm, v_hbm, mix_hbm, gm_hbm, query_hbm, ga_hbm, normed_hbm, wqkv_hbm, x_hbm,
    key_more, gain, down_bias, small_in, mid_hbm, gmid_hbm, ff_part, branch,
    out_hbm, tokens_hbm, qkv_sum, out_sum, up_sum, down_sum,
    gain_one, offset_one, qv_small, out_small, gain_two, offset_two, up_small, down_small,
    q_ref, k_ref, v_ref, mix_ref, gm_ref, query_more, ga_t, normed_t, wqkv, x_ref,
    out_ref, tokens_ref, key_t, key_acc, value_acc, dq, dk, dv, whole, mate, at_y, at_z, ff_y, ff_z, gn_own, gn_x,
    branch_x, branch_own, ff_own, held, small_own, small_z, small_y, small_c, small_x,
    bs, br, fys, fyr, fzs, fzr, acs, acr, ays, ayr, azs, azr, gs, gr, ls, ms, mr, os, hs, ins, more_ins, outs,
):
    length, width = x_ref.shape
    blocks = length // BLOCK
    strips = length // STRIP
    pairs = q_ref.shape[0]
    chunks = ff_part.shape[0]
    half = chunks // 2
    groups = chunks // GROUP
    me, head, core, y, across, core_mate, y_mate, z_mates = place()
    z = me // (Y_SIZE * CORES)
    by_pair = (
        (q_hbm, q_ref), (k_hbm, k_ref), (v_hbm, v_ref), (mix_hbm, mix_ref), (gm_hbm, gm_ref),
    )

    def pair_loads(p):
        both = pl.ds(2 * p, 2)
        first = p * (len(by_pair) + 1)
        return [
            pltpu.make_async_copy(src.at[p], dst.at[p], ins.at[first + n])
            for n, (src, dst) in enumerate(by_pair)
        ] + [
            pltpu.make_async_copy(
                query_hbm.at[both], query_more.at[both], ins.at[first + len(by_pair)]
            )
        ]

    late_loads = [
        pltpu.make_async_copy(src, dst, more_ins.at[n])
        for n, (src, dst) in enumerate(
            ((ga_hbm, ga_t), (normed_hbm, normed_t), (wqkv_hbm, wqkv), (x_hbm, x_ref))
        )
    ]
    for p in range(pairs):
        for copy in pair_loads(p):
            copy.start()
        if p == 0:
            late_loads[0].start()
            late_loads[1].start()
    late_loads[2].start()
    late_loads[3].start()
    greet([across, core_mate, y_mate, *z_mates])

    def part(b):
        return pl.ds(b * BLOCK, BLOCK)

    def branch_copy(b):
        return remote(branch.at[part(b), :], branch_x.at[part(b), :], bs.at[b], br.at[b], across)

    def load(n):
        source = mid_hbm if n < blocks else gmid_hbm
        return pltpu.make_async_copy(
            source.at[part(n % blocks), :], held.at[n % 2], ls.at[n % 2]
        )

    def taken(n):
        if n + 2 < 2 * blocks:
            load(n + 2).start()

    def group(g):
        return pl.ds(g * GROUP, GROUP)

    def ff_y_copy(g):
        return remote(
            ff_part.at[group(g), :, 1 - y], ff_y.at[group(g)], fys.at[g], fyr.at[g], y_mate
        )

    def ff_z_copy(g, d):
        n = g * 3 + d - 1
        return remote(
            ff_y.at[group(g), (z + d) % Z_SIZE], ff_z.at[d - 1, group(g)],
            fzs.at[n], fzr.at[n], z_mates[d - 1],
        )

    def branch_load(b):
        return pltpu.make_async_copy(branch.at[part(b), :], branch_own.at[b % 2], hs.at[b % 2])

    def ff_load(g):
        return pltpu.make_async_copy(
            ff_part.at[group(g), :, y], ff_own.at[g % 2], os.at[g % 2]
        )

    def ff_y_event(g):
        ff_y_copy(g).wait_recv()
        ff_load(g).wait()
        for n in range(g * GROUP, (g + 1) * GROUP):
            own = ff_own[g % 2, n % GROUP]
            ff_y[n] = (ff_y[n].astype(F32) + own.astype(F32)).astype(BF)
        if g + 2 < groups:
            ff_load(g + 2).start()
            ff_y_copy(g + 2).start()
        for d in (1, 2, 3):
            ff_z_copy(g, d).start()

    def ff_z_event(g):
        for d in (1, 2, 3):
            ff_z_copy(g, d).wait_recv()
        for n in range(g * GROUP, (g + 1) * GROUP):
            total = ff_y[n, z].astype(F32)
            for d in (1, 2, 3):
                total += ff_z[d - 1, n].astype(F32)
            if n < half:
                up_sum[:, n * CHUNK:(n + 1) * CHUNK] = total
            else:
                down_sum[:, (n - half) * CHUNK:(n - half + 1) * CHUNK] = total

    def at_c_copy(p):
        return remote(whole.at[p, :, :, 1 - core], mate.at[p], acs.at[p], acr.at[p], core_mate)

    def at_y_copy(p):
        return remote(mate.at[p, :, 1 - y], at_y.at[p], ays.at[p], ayr.at[p], y_mate)

    def at_z_copy(p, d):
        n = p * 3 + d - 1
        return remote(
            at_y.at[p, (z + d) % Z_SIZE], at_z.at[d - 1, p], azs.at[n], azr.at[n], z_mates[d - 1]
        )

    def at_c_event(p):
        at_c_copy(p).wait_recv()
        mate[p] = (mate[p].astype(F32) + whole[p, :, :, core].astype(F32)).astype(BF)
        at_y_copy(p).start()

    def at_y_event(p):
        at_y_copy(p).wait_recv()
        at_y[p] = (at_y[p].astype(F32) + mate[p, :, y].astype(F32)).astype(BF)
        for d in (1, 2, 3):
            at_z_copy(p, d).start()

    def at_z_event(p):
        for d in (1, 2, 3):
            at_z_copy(p, d).wait_recv()
        total = at_y[p, z].astype(F32)
        for d in (1, 2, 3):
            total += at_z[d - 1, p].astype(F32)
        cut = slice(p * PAIR, (p + 1) * PAIR)
        for kind in range(3):
            qkv_sum[kind, :, cut] = total[:, kind * PAIR:(kind + 1) * PAIR]
        out_sum[:, cut] = total[:, 3 * PAIR:]

    def out_copy(b):
        return pltpu.make_async_copy(out_ref.at[part(b), :], out_hbm.at[part(b), :], outs.at[b])

    def tokens_copy(b):
        return pltpu.make_async_copy(
            tokens_ref.at[part(b), :], tokens_hbm.at[part(b), :], outs.at[blocks + b]
        )

    def branch_event(b):
        branch_copy(b).wait_recv()
        load(b).wait()
        branch_load(b).wait()
        both = branch_own[b % 2].astype(F32) + branch_x[part(b), :].astype(F32)
        out_ref[part(b), :] = (held[b % 2] + both + as_row(down_bias)).astype(BF)
        out_copy(b).start()
        taken(b)
        if b + 2 < blocks:
            branch_load(b + 2).start()

    for b in range(blocks):
        branch_copy(b).start()
    for n in range(2):
        load(n).start()
        branch_load(n).start()
        ff_load(n).start()
        ff_y_copy(n).start()

    plan = {
        2: [(at_c_event, 0), (ff_y_event, 0), (branch_event, 0)], 4: [(at_c_event, 1)],
        5: [(ff_y_event, 1), (branch_event, 1)], 6: [(at_c_event, 2)],
    }

    low_lanes = lanes() < HEAD_DIM
    zero = jnp.zeros((1, PAIR), BF)

    def stacked(strip):
        return jnp.concatenate(
            [jnp.where(low_lanes, strip, zero), jnp.where(low_lanes, zero, strip)], axis=0
        )

    def attend(t, _):
        p, b = t // strips, t % strips
        rows = pl.ds(pl.multiple_of(b * STRIP, STRIP), STRIP)

        @pl.when(b == 0)
        def _():
            for p_now in range(pairs):
                @pl.when(p == p_now)
                def _(p_now=p_now):
                    for copy in pair_loads(p_now):
                        copy.wait()
            key_t[...] = turn(k_ref[p])
            key_acc[...] = jnp.zeros_like(key_acc)
            value_acc[...] = jnp.zeros_like(value_acc)

        queries, grads = stacked(q_ref[p, rows, :]), stacked(gm_ref[p, rows, :])
        more = jnp.concatenate(
            [query_more[2 * p, rows, :], query_more[2 * p + 1, rows, :]], axis=0
        )
        mixture = mix_ref[p, rows, :]
        product = grads.astype(F32) * jnp.concatenate([mixture, mixture], axis=0).astype(F32)
        inner = -jnp.sum(product, axis=-1, keepdims=True)
        query_side = jnp.concatenate([queries, more], axis=1)
        grad_side = jnp.concatenate([grads, in_pieces(inner, 0, 0.0)], axis=1)
        to_queries = jnp.zeros((PAIR, 2 * STRIP), F32)
        for n in range(blocks):
            keys = jnp.concatenate([k_ref[p, part(n), :], key_more[part(n), :]], axis=1)
            values = jnp.concatenate([v_ref[p, part(n), :], one_lanes(BLOCK)], axis=1)
            weights = jnp.exp(dot_rows(keys, query_side)).astype(BF)
            grad_scores = weights * dot_rows(values, grad_side).astype(BF)
            value_acc[part(n), :] += split_sum(weights, grads)
            key_acc[part(n), :] += split_sum(grad_scores, queries)
            to_queries += nn(key_t[:, part(n)], grad_scores)
        own = jnp.concatenate(
            [to_queries[:HEAD_DIM, :STRIP], to_queries[HEAD_DIM:, STRIP:]], axis=0
        )
        dq[p, rows, :] = (turn(own) * 0.125).astype(BF)

        @pl.when(b == strips - 1)
        def _():
            @pl.when(p == 0)
            def _():
                late_loads[0].wait()
                late_loads[1].wait()

            dk[p] = key_acc[...].astype(BF)
            dv[p] = value_acc[...].astype(BF)
            right = jnp.concatenate([dq[p], dk[p], dv[p]], axis=1)
            mixture_all = mix_ref[p]

            def one(plane, _):
                cut = pl.ds(pl.multiple_of(plane * BLOCK, BLOCK), BLOCK)
                both = jnp.concatenate(
                    [nn(normed_t[cut, :], right), nn(ga_t[cut, :], mixture_all)], axis=1
                )
                whole[p, plane] = both.astype(BF).reshape(whole.shape[2:])
                return 0

            lax.fori_loop(0, Z_SIZE, one, 0)
            at_c_copy(p).start()

        for step, events in plan.items():
            @pl.when(t == step)
            def _(events=events):
                for event, n in events:
                    event(n)
        return 0

    lax.fori_loop(0, pairs * strips, attend, 0)
    late_loads[2].wait()
    late_loads[3].wait()

    def gn_copy(b):
        return remote(gn_own.at[b], gn_x.at[b], gs.at[b], gr.at[b], across)

    own_gain = jnp.zeros((1, width), F32)
    own_offset = jnp.zeros((1, width), F32)
    for b in range(blocks):
        total = jnp.zeros((BLOCK, width), F32)
        for n, grad in enumerate((dq, dk, dv)):
            left = jnp.concatenate([grad[p, part(b), :] for p in range(pairs)], axis=1)
            total += dot_rows(left, wqkv[n])
        gn_own[b] = total.astype(BF)
        gn_copy(b).start()
        centred, scale = norm_stats(x_ref[part(b), :].astype(F32))
        own_gain += sum_rows(total * (centred * scale))
        own_offset += sum_rows(total)

    at_c_event(3)
    small_own[...] = small_in[...]
    small_own[LN1_GAIN:LN1_GAIN + 1, :] = own_gain
    small_own[LN1_BIAS:LN1_BIAS + 1, :] = own_offset
    for p in range(pairs):
        first, second = p * PAIR, (pairs + p) * PAIR
        small_own[QV_BIAS:QV_BIAS + 1, first:first + PAIR] = sum_rows(dq[p].astype(F32))
        small_own[QV_BIAS:QV_BIAS + 1, second:second + PAIR] = sum_rows(dv[p].astype(F32))
    def small_z_copy(d):
        return remote(small_own, small_z.at[z], ms.at[d - 1], mr.at[d - 1], z_mates[d - 1])

    def small_z_arrival(d):
        slot = small_z.at[(z + Z_SIZE - d) % Z_SIZE]
        return remote(slot, slot, ms.at[d - 1], mr.at[d - 1], z_mates[d - 1])

    y_sum = remote(small_y.at[0], small_y.at[1], ms.at[3], mr.at[3], y_mate)
    c_sum = remote(small_c.at[0], small_c.at[1], ms.at[4], mr.at[4], core_mate)
    x_sum = remote(small_x.at[0], small_x.at[1], ms.at[5], mr.at[5], across)
    for d in (1, 2, 3):
        small_z_copy(d).start()
    small_z[z] = small_own[...]

    def small_y_step():
        for d in (1, 2, 3):
            small_z_arrival(d).wait_recv()
        small_y[0] = small_z[0] + small_z[1] + small_z[2] + small_z[3]
        y_sum.start()

    def small_c_step():
        y_sum.wait()
        small_c[0] = small_y[0] + small_y[1]
        c_sum.start()

    def small_x_step():
        c_sum.wait()
        small_x[0] = small_c[0, 0:8, :] + small_c[1, 0:8, :]
        x_sum.start()

    branch_event(2)
    ff_y_event(2)
    branch_event(3)
    ff_z_event(0)
    ff_y_event(3)
    at_y_event(0)
    ff_z_event(1)
    gains = as_row(gain)
    for b in range(blocks):
        gn_copy(b).wait()
        load(blocks + b).wait()
        grad = gn_own[b].astype(F32) + gn_x[b].astype(F32)
        centred, scale = norm_stats(x_ref[part(b), :].astype(F32))
        unit = centred * scale
        tokens_ref[part(b), :] = (
            held[b % 2] + norm_back(grad * gains, unit, scale)
        ).astype(BF)
        tokens_copy(b).start()
        taken(blocks + b)
        if b == 0:
            small_y_step()
            at_y_event(1)
            at_y_event(2)
            ff_z_event(2)
        if b == 1:
            small_c_step()
            at_y_event(3)
            ff_z_event(3)
        if b == 2:
            small_x_step()
            at_z_event(0)
            at_z_event(1)
            at_z_event(2)

    at_z_event(3)
    x_sum.wait()
    ln1 = small_x[0, 0:2, :] + small_x[1, 0:2, :]
    gain_one[...] = ln1[0:1, :].reshape(width)
    offset_one[...] = ln1[1:2, :].reshape(width)
    small = small_c[0] + small_c[1]
    for kind, target in (
        (OUT_BIAS, out_small), (LN2_GAIN, gain_two), (LN2_BIAS, offset_two), (DOWN_BIAS, down_small),
    ):
        target[...] = small[kind:kind + 1, :].reshape(width)
    cols = pairs * PAIR
    qv_small[0:1, :] = small[QV_BIAS:QV_BIAS + 1, :cols]
    qv_small[1:2, :] = small[QV_BIAS:QV_BIAS + 1, cols:]
    for n in range(up_small.shape[0] // width):
        row = small[UP_BIAS + n:UP_BIAS + n + 1, :]
        up_small[n * width:(n + 1) * width] = row.reshape(width)

    for d in (1, 2, 3):
        small_z_copy(d).wait_send()
    for b in range(blocks):
        out_copy(b).wait()
        tokens_copy(b).wait()
        branch_copy(b).wait_send()
    for g in range(groups):
        ff_y_copy(g).wait_send()
        for d in (1, 2, 3):
            ff_z_copy(g, d).wait_send()
    for p in range(pairs):
        at_c_copy(p).wait_send()
        at_y_copy(p).wait_send()
        for d in (1, 2, 3):
            at_z_copy(p, d).wait_send()


def run_back(
    queries, keys, values, mixture, grad_mixture, query_more, ga_t, normed_t, wqkv, x,
    key_more, gain, down_bias, small, middle, grad_middle, ff_part, branch,
):
    length, width = x.shape
    pairs = queries.shape[0]
    chunks, depth = ff_part.shape[0], ff_part.shape[3]
    groups = chunks // GROUP
    cols, hidden = pairs * PAIR, chunks // 2 * CHUNK
    blocks = length // BLOCK
    dma = pltpu.SemaphoreType.DMA
    rows = pltpu.VMEM((blocks, BLOCK, width), BF)
    by_pair = pltpu.VMEM((pairs, length, PAIR), BF)
    whole_rows = pltpu.VMEM((length, width), BF)
    row = shape_of((width,), F32)
    loaded = (
        queries, keys, values, mixture, grad_mixture, query_more, ga_t, normed_t, wqkv, x
    )
    return pl.pallas_call(
        back_kernel,
        out_shape=[
            shape_of((length, width), BF),
            shape_of((length, width), BF),
            shape_of((3, depth, cols), F32),
            shape_of((depth, cols), F32),
            shape_of((depth, hidden), F32),
            shape_of((depth, hidden), F32),
            row, row, shape_of((2, cols), F32), row, row, row, shape_of((hidden,), F32), row,
        ],
        in_specs=[ANY_SPEC] * 10 + [VMEM_SPEC] * 4 + [ANY_SPEC] * 4,
        out_specs=[ANY_SPEC] * 2 + [VMEM_SPEC] * 12,
        scratch_shapes=[pltpu.VMEM(v.shape, BF) for v in loaded] + [
            whole_rows, whole_rows, pltpu.VMEM((PAIR, length), BF),
            pltpu.VMEM((length, PAIR), F32), pltpu.VMEM((length, PAIR), F32),
            by_pair, by_pair, by_pair,
            pltpu.VMEM((pairs, Z_SIZE, Y_SIZE, CORES, depth, CHUNK), BF),
            pltpu.VMEM((pairs, Z_SIZE, Y_SIZE, depth, CHUNK), BF),
            pltpu.VMEM((pairs, Z_SIZE, depth, CHUNK), BF),
            pltpu.VMEM((3, pairs, depth, CHUNK), BF),
            pltpu.VMEM((chunks, Z_SIZE, depth, CHUNK), BF),
            pltpu.VMEM((3, chunks, depth, CHUNK), BF),
            rows, rows, whole_rows,
            pltpu.VMEM((2, BLOCK, width), BF),
            pltpu.VMEM((2, GROUP, Z_SIZE, depth, CHUNK), BF),
            pltpu.VMEM((2, BLOCK, width), F32),
            pltpu.VMEM(small.shape, F32),
            pltpu.VMEM((Z_SIZE,) + small.shape, F32),
            pltpu.VMEM((2,) + small.shape, F32),
            pltpu.VMEM((2,) + small.shape, F32),
            pltpu.VMEM((2, 8, width), F32),
            dma((blocks,)), dma((blocks,)), dma((groups,)), dma((groups,)),
            dma((3 * groups,)), dma((3 * groups,)), dma((pairs,)), dma((pairs,)),
            dma((pairs,)), dma((pairs,)), dma((3 * pairs,)), dma((3 * pairs,)),
            dma((blocks,)), dma((blocks,)), dma((2,)), dma((6,)), dma((6,)), dma((2,)), dma((2,)),
            dma((6 * pairs,)), dma((4,)), dma((2 * blocks,)),
        ],
        compiler_params=pltpu.CompilerParams(
            collective_id=2, has_side_effects=True, vmem_limit_bytes=VMEM_LIMIT
        ),
    )(*loaded, key_more, gain, down_bias, small, middle, grad_middle, ff_part, branch)


def hand_over_kernel(*refs):
    *refs, sems = refs
    count = len(refs) // 3
    refs = refs[:count] + refs[2 * count:] + refs[count:2 * count]
    loads, stores = (
        [
            pltpu.make_async_copy(refs[a * count + n], refs[b * count + n], sems.at[a, n])
            for n in range(count)
        ]
        for a, b in ((0, 1), (1, 2))
    )
    for load in loads:
        load.start()
    for load, store in zip(loads, stores):
        load.wait()
        store.start()
    for store in stores:
        store.wait()


def hand_over(results):
    return pl.pallas_call(
        hand_over_kernel,
        out_shape=[shape_of(v.shape, v.dtype) for v in results],
        in_specs=[ANY_SPEC] * len(results),
        out_specs=[ANY_SPEC] * len(results),
        scratch_shapes=[pltpu.VMEM(v.shape, v.dtype) for v in results] + [
            pltpu.SemaphoreType.DMA((2, len(results)))
        ],
        compiler_params=pltpu.CompilerParams(vmem_limit_bytes=VMEM_LIMIT),
    )(*results)


def fast_body(
    tokens, segment_ids, context_flags, ln1_gain, ln1_bias, qkv_weight, qv_bias, out_weight,
    out_bias, ln2_gain, ln2_bias, up_weight, up_bias, down_weight, down_bias, cotangent,
):
    x, dy = tokens[0], cotangent[0]
    (
        queries, keys, values, mixture, middle, normed_t, wff, key_more, query_more,
        normed_two_t, active, slope,
    ) = run_fwd(
        x, segment_ids, context_flags, ln1_gain, ln1_bias, qv_bias, out_bias, ln2_gain,
        ln2_bias, up_bias, qkv_weight, out_weight, up_weight, down_weight.T,
    )
    branch, grad_middle, ga_t, grad_mixture, ff_part, small = run_ff(
        middle, dy, wff, normed_two_t, active, slope, ln2_gain, out_weight
    )
    (
        output, tokens_grad, qkv_grad, out_grad, up_grad, down_grad, gain_one, offset_one,
        qv_grad, out_bias_grad, gain_two, offset_two, up_bias_grad, down_bias_grad,
    ) = hand_over(run_back(
        queries, keys, values, mixture, grad_mixture, query_more, ga_t, normed_t, qkv_weight, x,
        key_more, ln1_gain, down_bias, small, middle, grad_middle, ff_part, branch,
    ))
    return (
        output[None], tokens_grad[None], gain_one, offset_one, qkv_grad, qv_grad, out_grad.T,
        out_bias_grad, gain_two, offset_two, up_grad, up_bias_grad, down_grad.T, down_bias_grad,
    )


def solution(mesh):
    chosen = generic_body
    if mesh.shape["head"] == 2 and mesh.shape["seq"] == SEQ_SIZE:
        chosen = fast_body
    return jax.shard_map(
        chosen,
        mesh=mesh,
        in_specs=(
            P("seq", None, None),
            P("seq", None),
            P("seq", None),
            P(),
            P(),
            P(None, None, "head"),
            P(None, "head"),
            P("head", None),
            P(),
            P(),
            P(),
            P("seq", "head"),
            P("head"),
            P("head", "seq"),
            P(),
            P("seq", None, None),
        ),
        out_specs=(
            P("seq", None, None),
            P("seq", None, None),
            P(),
            P(),
            P(None, "seq", "head"),
            P(None, "head"),
            P("head", "seq"),
            P(),
            P(),
            P(),
            P("seq", "head"),
            P("head"),
            P("head", "seq"),
            P(),
        ),
        check_vma=False,
    )
```

profile of v0, /device:TPU:0, one launch (start us, length us, event | category | flops | bytes accessed | tf_op | source)
XLA Modules:
  0.0 226.8 jit_solution(14720905920251817172)
XLA Ops:
  0.6 66.5 %shard_map.263 = (bf16[4,1024,128]{2,1,0:T(8,128)(2,1)}, bf16[4,1024,128]{2,1,0:T(8,128)(2,1)}, bf16[4,1024,128]{2,1,0:T(8,128)(2,1)}, bf16[4,1024,128]{2,1,0:T(...) custom-call(bf16[1024,1024]{1,0:T(8,128)(2,1)} %bitcast.7, ...), custom_call_target="tpu_custom_call" | custom-call | tf_op jit(solution)/shard_map/pallas_call | solution.py:737
  67.2 55.5 %shard_map.264 = (bf16[1024,1024]{1,0:T(8,128)(2,1)}, f32[1024,1024]{1,0:T(8,128)}, bf16[1024,1024]{1,0:T(8,128)(2,1)}, bf16[4,1024,128]{2,1,0:T(8,128)(2,1)}, b...) custom-call(f32[1024,1024]{1,0:T(8,128)} %get-tuple-element.64.mid_hbm, bf16[1024,1024]{1,0:T(8,128)(2,1)} %bitcast.9, ...), custom_call_target="tpu_custom_call" | custom-call | tf_op jit(solution)/shard_map/pallas_call | solution.py:996
  122.7 99.6 %shard_map.265 = (bf16[1024,1024]{1,0:T(8,128)(2,1)}, bf16[1024,1024]{1,0:T(8,128)(2,1)}, f32[3,64,512]{2,1,0:T(8,128)}, f32[64,512]{1,0:T(8,128)}, f32[64,2048]...) custom-call(bf16[4,1024,128]{2,1,0:T(8,128)(2,1)} %get-tuple-element, ...), custom_call_target="tpu_custom_call" | custom-call | tf_op jit(solution)/shard_map/pallas_call | solution.py:1426
  222.3 4.4 %shard_map.266 = (bf16[1024,1024]{1,0:T(8,128)(2,1)}, bf16[1024,1024]{1,0:T(8,128)(2,1)}, f32[3,64,512]{2,1,0:T(8,128)}, f32[64,512]{1,0:T(8,128)}, f32[64,2048]...) custom-call(bf16[1024,1024]{1,0:T(8,128)(2,1)} %get-tuple-element.78, ...), custom_call_target="tpu_custom_call" | custom-call | tf_op jit(solution)/shard_map/pallas_call | solution.py:1491
where the time goes:
time: 227 us
  Pallas kernels  226 us (100%)
    pallas_call x1, Pallas kernels, run_back(): pl.pallas_call(back_kernel, out_shape=[shape_of((length, width), BF), sha...  99.6 us
    pallas_call x1, Pallas kernels, run_fwd(): pl.pallas_call(fwd_kernel, out_shape=[shape_of(by_pair, BF)] * 4 + [shape...  66.5 us
    pallas_call x1, Pallas kernels, run_ff(): pl.pallas_call(ff_kernel, out_shape=[shape_of((length, width), BF), shape...  55.5 us

commit v1 on v0

--- a/solution.py
+++ b/solution.py
@@ -409,12 +409,11 @@
 
 
 def fwd_kernel(
-    x_ref, seg_ref, context, gain, offset, qv_bias, out_bias, gain_two, offset_two, up_bias,
+    x_ref, seg_ref, context, gain, offset, qv_bias, out_bias,
     wqkv, wout, up_shard, down_shard,
     q_out, k_out, v_out, mix_out, mid_out, normed_out, wff_out, key_out, query_out,
-    normed_two_out, active_out, slope_out,
     wff, q_ref, k_ref, v_ref, mix_ref, mid_ref, normed_t, key_more, query_more,
-    normed_two_t, active, slope, bias_row, mask_more, wout_x, mix_x,
+    mask_more, wout_all, mix_x,
     zs, zr, ys, yr, cs, cr, xs, xr, local, outs,
 ):
     length, width = x_ref.shape
@@ -436,7 +435,11 @@
     half = wout.shape[0] // 2
     here = pl.ds(pl.multiple_of(core * half, half), half)
     beside = pl.ds(pl.multiple_of((1 - core) * half, half), half)
-    out_copy = remote(wout.at[here, :], wout_x.at[here, :], xs.at[0], xr.at[0], across)
+    wout_x = wout_all.at[1 - head]
+    out_copy = remote(
+        wout.at[here, :], wout_all.at[head, here, :], xs.at[0], xr.at[0], across
+    )
+    wout_all[head] = wout[...]
     out_pass = remote(wout_x.at[here, :], wout_x.at[here, :], cs.at[28], cr.at[28], core_mate)
     out_arrival = remote(
         wout_x.at[beside, :], wout_x.at[beside, :], cs.at[28], cr.at[28], core_mate
@@ -636,37 +639,6 @@
         rows = pl.ds(b * BLOCK, BLOCK)
         return pltpu.make_async_copy(mid_ref.at[rows, :], mid_out.at[rows, :], outs.at[7 + b])
 
-    gains_two, offsets_two = as_row(gain_two), as_row(offset_two)
-    bias_row[...] = as_row(up_bias)
-
-    def half_copies(b):
-        rows = pl.ds(b * BLOCK, BLOCK)
-        return [
-            pltpu.make_async_copy(
-                here.at[:, rows, :], there.at[:, rows, :], outs.at[7 + blocks + 2 * b + n]
-            )
-            for n, (here, there) in enumerate(((active, active_out), (slope, slope_out)))
-        ]
-
-    def up_half(b):
-        rows = pl.ds(b * BLOCK, BLOCK)
-        centred, scale = norm_stats(mid_ref[rows, :])
-        block = (centred * scale * gains_two + offsets_two).astype(BF)
-        normed_two_t[:, rows] = turn(block)
-
-        def one(n, _):
-            cut = pl.ds(pl.multiple_of(n * WIDE, WIDE), WIDE)
-            before = nn(block, wff[0, :, :, cut].reshape(width, WIDE)) + bias_row[:, cut]
-            spread = 0.5 * (1.0 + lax.erf(before * INV_ROOT_TWO))
-            active[n, rows, :] = (before * spread).astype(BF)
-            bell = INV_ROOT_TWO_PI * jnp.exp(before * before * -0.5)
-            slope[n, rows, :] = (spread + before * bell).astype(BF)
-            return 0
-
-        lax.fori_loop(0, active.shape[0], one, 0)
-        for copy in half_copies(b):
-            copy.start()
-
     def arrive(u):
         for f in range(len(flows)):
             def one(f=f):
@@ -681,29 +653,21 @@
         rows = pl.ds(b * BLOCK, BLOCK)
         ours = jnp.concatenate([mix_ref[p, rows, :] for p in range(pairs)], axis=-1)
         other = jnp.concatenate([mix_x[p, rows, :] for p in range(pairs)], axis=-1)
-        attended = nn(ours, wout[...]) + nn(other, wout_x[...])
+        first, second = jnp.where(head == 0, ours, other), jnp.where(head == 0, other, ours)
+        attended = nn(first, wout_all[0]) + nn(second, wout_all[1])
         mid_ref[rows, :] = x_ref[rows, :].astype(F32) + (attended + out_row)
         mid_copy(b).start()
-        if b == 0:
-            arrive(0)
-        up_half(b)
         if b < 3:
             y_event(1, b + 1)
-    normed_two_keep = pltpu.make_async_copy(
-        normed_two_t, normed_two_out, outs.at[7 + 3 * blocks]
-    )
-    normed_two_keep.start()
     wff_keep = [pltpu.make_async_copy(wff.at[u], wff_out.at[u], local.at[u]) for u in range(2)]
+    arrive(0)
     wff_keep[0].start()
     arrive(1)
     wff_keep[1].start()
     out_copy.wait_send()
     out_pass.wait_send()
-    for copy in keep + wff_keep + [normed_two_keep]:
+    for copy in keep + wff_keep:
         copy.wait()
-    for b in range(blocks):
-        for copy in half_copies(b):
-            copy.wait()
     for t in range(length // STRIP * pairs):
         mixture_copy(t).wait_send()
     for b in range(blocks):
@@ -721,17 +685,13 @@
             for_flow(f, finish)
 
 
-def run_fwd(
-    x, seg, context, gain, offset, qv_bias, out_bias, gain_two, offset_two, up_bias, wqkv, wout,
-    up_weight, down_t,
-):
+def run_fwd(x, seg, context, gain, offset, qv_bias, out_bias, wqkv, wout, up_weight, down_t):
     length, width = x.shape
     pairs = wqkv.shape[2] // PAIR
     blocks = length // BLOCK
     depth, hidden = up_weight.shape
     by_pair, by_head = (pairs, length, PAIR), (2 * pairs, length, PAIR)
     turned = (width, length)
-    halves = (hidden // WIDE, length, WIDE)
     steps = length // STRIP * pairs
     dma = pltpu.SemaphoreType.DMA
     return pl.pallas_call(
@@ -742,46 +702,36 @@
             shape_of((2, SEQ_SIZE, depth, hidden), BF),
             shape_of((length, PAIR), BF),
             shape_of(by_head, BF),
-            shape_of((width, length), BF),
-            shape_of(halves, BF),
-            shape_of(halves, BF),
         ],
-        in_specs=[VMEM_SPEC] * 12 + [ANY_SPEC] * 2,
-        out_specs=[ANY_SPEC] * 12,
+        in_specs=[VMEM_SPEC] * 9 + [ANY_SPEC] * 2,
+        out_specs=[ANY_SPEC] * 9,
         scratch_shapes=[pltpu.VMEM((2, SEQ_SIZE, depth, hidden), BF)]
         + [pltpu.VMEM(by_pair, BF)] * 4 + [
             pltpu.VMEM((length, width), F32),
             pltpu.VMEM(turned, BF),
             pltpu.VMEM((length, PAIR), BF),
             pltpu.VMEM(by_head, BF),
-            pltpu.VMEM((width, length), BF),
-            pltpu.VMEM(halves, BF),
-            pltpu.VMEM(halves, BF),
-            pltpu.VMEM((1, hidden), F32),
             pltpu.VMEM((length, PAIR), BF),
-            pltpu.VMEM(wout.shape, BF),
+            pltpu.VMEM((2,) + wout.shape, BF),
             pltpu.VMEM(by_pair, BF),
             dma((12,)), dma((12,)), dma((14,)), dma((14,)), dma((29,)), dma((29,)),
-            dma((1 + steps,)), dma((1 + steps,)), dma((2,)), dma((8 + 3 * blocks,)),
+            dma((1 + steps,)), dma((1 + steps,)), dma((2,)), dma((7 + blocks,)),
         ],
         compiler_params=pltpu.CompilerParams(
             collective_id=0, has_side_effects=True, vmem_limit_bytes=VMEM_LIMIT
         ),
-    )(
-        x, seg, context, gain, offset, qv_bias, out_bias, gain_two, offset_two, up_bias, wqkv,
-        wout, up_weight, down_t,
-    )
+    )(x, seg, context, gain, offset, qv_bias, out_bias, wqkv, wout, up_weight, down_t)
 
 
 def ff_kernel(
-    mid_hbm, dy_hbm, wff_hbm, normed_two_hbm, active_hbm, slope_hbm, gain, wout_hbm,
+    mid_hbm, dy_hbm, wff_hbm, gain, offset, up_bias, wout_hbm,
     branch_out, gmid_hbm, ga_out, gm_out, summed, small_ref,
-    dy_ref, wff, wout, branch_ref, ga_t, gm_ref, normed_t, dy_t, active, before_grad, gnt_acc, gnt_own, gnt_x, whole, from_mate,
+    dy_ref, wff, wout, bias_row, branch_ref, ga_t, gm_ref, normed, normed_t, dy_t, active, before_grad, gnt_acc, gnt_own, gnt_x, whole, from_mate,
     held, ready,
     xs, xr, cs, cr, ls, ws, ss, ins, outs,
 ):
     length, width = dy_ref.shape
-    blocks = length // BLOCK
+    blocks = length // PIECE
     hidden = wff.shape[3]
     half = hidden // WIDE
     chunks = 2 * hidden // CHUNK
@@ -790,30 +740,19 @@
     dy_load = pltpu.make_async_copy(dy_hbm, dy_ref, ins.at[0])
     wout_load = pltpu.make_async_copy(wout_hbm, wout, ins.at[1])
 
-    def step_loads(n):
+    def wff_load(n):
         cut = pl.ds(n * WIDE, WIDE)
-        return [
-            pltpu.make_async_copy(src, dst, ins.at[4 + 3 * n + m])
-            for m, (src, dst) in enumerate(
-                (
-                    (wff_hbm.at[1, :, :, cut], wff.at[1, :, :, cut]),
-                    (slope_hbm.at[n], before_grad.at[n]),
-                    (wff_hbm.at[0, :, :, cut], wff.at[0, :, :, cut]),
-                )
-            )
-        ]
-
-    active_load = pltpu.make_async_copy(active_hbm, active, ins.at[2])
-    normed_load = pltpu.make_async_copy(normed_two_hbm, normed_t, ins.at[3])
+        return pltpu.make_async_copy(
+            wff_hbm.at[:, :, :, cut], wff.at[:, :, :, cut], ins.at[2 + n]
+        )
+
     dy_load.start()
     for n in range(half):
-        for copy in step_loads(n):
-            copy.start()
-    active_load.start()
-    normed_load.start()
+        wff_load(n).start()
     wout_load.start()
     greet([across, core_mate])
-    gains = as_row(gain)
+    gains, offsets = as_row(gain), as_row(offset)
+    bias_row[...] = as_row(up_bias)
 
     def weight(kind, n):
         cut = pl.ds(pl.multiple_of(n * WIDE, WIDE), WIDE)
@@ -821,12 +760,12 @@
 
     small_ref[...] = jnp.zeros_like(small_ref)
 
-    def load(b):
-        rows = pl.ds(b * BLOCK, BLOCK)
-        return pltpu.make_async_copy(mid_hbm.at[rows, :], held.at[b % 2], ls.at[b % 2])
+    def load(n):
+        rows = pl.ds(n % blocks * PIECE, PIECE)
+        return pltpu.make_async_copy(mid_hbm.at[rows, :], held.at[n % 2], ls.at[n % 2])
 
     def store(b):
-        rows = pl.ds(b * BLOCK, BLOCK)
+        rows = pl.ds(b * PIECE, PIECE)
         return pltpu.make_async_copy(ready.at[b % 2], gmid_hbm.at[rows, :], ws.at[b % 2])
 
     load(0).start()
@@ -842,24 +781,36 @@
 
     def forward(t, _):
         b, n = t // half, t % half
-        rows = pl.ds(pl.multiple_of(b * BLOCK, BLOCK), BLOCK)
+        rows = pl.ds(pl.multiple_of(b * PIECE, PIECE), PIECE)
+
+        for b_next in range(blocks):
+            @pl.when(t == b_next * half)
+            def _(b_next=b_next):
+                load(b_next).wait()
+                if b_next == 0:
+                    dy_load.wait()
 
         for n_first in range(half):
             @pl.when(t == n_first)
             def _(n_first=n_first):
-                if n_first == 0:
-                    dy_load.wait()
-                for copy in step_loads(n_first):
-                    copy.wait()
+                wff_load(n_first).wait()
 
         @pl.when(n == 0)
         def _():
+            centred, scale = norm_stats(held[b % 2])
+            block = (centred * scale * gains + offsets).astype(BF)
+            normed[...] = block
+            normed_t[:, rows] = turn(block)
             dy_t[:, rows] = turn(dy_ref[rows, :])
             small_ref[DOWN_BIAS:DOWN_BIAS + 1, :] += sum_rows(dy_ref[rows, :].astype(F32))
 
         up = weight(0, n)
-        grad = nn(dy_ref[rows, :], weight(1, n)) * before_grad[n, rows, :].astype(F32)
-        grad = grad.astype(BF)
+        cut = pl.ds(pl.multiple_of(n * WIDE, WIDE), WIDE)
+        before = nn(normed[...], up) + bias_row[:, cut]
+        spread = 0.5 * (1.0 + lax.erf(before * INV_ROOT_TWO))
+        active[n, rows, :] = (before * spread).astype(BF)
+        slope = spread + before * (INV_ROOT_TWO_PI * jnp.exp(before * before * -0.5))
+        grad = (nn(dy_ref[rows, :], weight(1, n)) * slope).astype(BF)
         before_grad[n, rows, :] = grad
         small_ref[pl.ds(UP_BIAS + n, 1), :] += sum_rows(grad.astype(F32))
         back = dot_rows(grad, up)
@@ -875,6 +826,7 @@
         for b_done in range(blocks):
             @pl.when(t == (b_done + 1) * half - 1)
             def _(b_done=b_done):
+                load(b_done + 2).start()
                 gnt_own[b_done] = gnt_acc[...].astype(BF)
                 gnt_copy(b_done).start()
         return 0
@@ -902,8 +854,6 @@
 
         lax.fori_loop(0, Z_SIZE * half, one, 0)
 
-    active_load.wait()
-    normed_load.wait()
     weight_grads(dy_t, active, chunks // 2)
     weight_grads(normed_t, before_grad, 0)
 
@@ -915,17 +865,17 @@
         branch_ref[rows, :] = total.astype(BF)
         return 0
 
-    lax.fori_loop(0, blocks, branch, 0)
+    lax.fori_loop(0, length // BLOCK, branch, 0)
     branch_keep = pltpu.make_async_copy(branch_ref, branch_out, outs.at[0])
     branch_keep.start()
     wout_load.wait()
 
     def ga_copy(b):
-        rows = pl.ds(b * BLOCK, BLOCK)
+        rows = pl.ds(b * PIECE, PIECE)
         return pltpu.make_async_copy(ga_t.at[:, rows], ga_out.at[:, rows], outs.at[1 + b])
 
     def gm_copy(b):
-        rows = pl.ds(b * BLOCK, BLOCK)
+        rows = pl.ds(b * PIECE, PIECE)
         return pltpu.make_async_copy(
             gm_ref.at[:, rows, :], gm_out.at[:, rows, :], outs.at[1 + blocks + b]
         )
@@ -942,37 +892,33 @@
     keep = pltpu.make_async_copy(from_mate, summed, ss.at[0])
     keep.start()
 
-    strips = BLOCK // PIECE
+    def through_norm(b):
+        rows = pl.ds(b * PIECE, PIECE)
+        grad = gnt_own[b].astype(F32) + gnt_x[b].astype(F32)
+        centred, scale = norm_stats(held[b % 2])
+        unit = centred * scale
+        small_ref[LN2_GAIN:LN2_GAIN + 1, :] += sum_rows(grad * unit)
+        small_ref[LN2_BIAS:LN2_BIAS + 1, :] += sum_rows(grad)
+        total = dy_ref[rows, :].astype(F32) + norm_back(grad * gains, unit, scale)
+        ready[b % 2] = total
+        low = total.astype(BF)
+        small_ref[OUT_BIAS:OUT_BIAS + 1, :] += sum_rows(low.astype(F32))
+        ga_t[:, rows] = turn(low)
+        mixed = dot_rows(low, wout[...]).astype(BF)
+        for p in range(pairs):
+            gm_ref[p, rows, :] = mixed[:, p * PAIR:(p + 1) * PAIR]
+
     for b in range(blocks):
         gnt_copy(b).wait()
-        load(b).wait()
+        load(blocks + b).wait()
         if b >= 2:
             store(b - 2).wait()
-
-        def through_norm(n, _, b=b):
-            rows = pl.ds(pl.multiple_of(n * PIECE, PIECE), PIECE)
-            full = pl.ds(pl.multiple_of(b * BLOCK + n * PIECE, PIECE), PIECE)
-            grad = gnt_own[b, rows, :].astype(F32) + gnt_x[b, rows, :].astype(F32)
-            centred, scale = norm_stats(held[b % 2, rows, :])
-            unit = centred * scale
-            small_ref[LN2_GAIN:LN2_GAIN + 1, :] += sum_rows(grad * unit)
-            small_ref[LN2_BIAS:LN2_BIAS + 1, :] += sum_rows(grad)
-            total = dy_ref[full, :].astype(F32) + norm_back(grad * gains, unit, scale)
-            ready[b % 2, rows, :] = total
-            low = total.astype(BF)
-            small_ref[OUT_BIAS:OUT_BIAS + 1, :] += sum_rows(low.astype(F32))
-            ga_t[:, full] = turn(low)
-            mixed = dot_rows(low, wout[...]).astype(BF)
-            for p in range(pairs):
-                gm_ref[p, full, :] = mixed[:, p * PAIR:(p + 1) * PAIR]
-            return 0
-
-        lax.fori_loop(0, strips, through_norm, 0)
+        through_norm(b)
         store(b).start()
         ga_copy(b).start()
         gm_copy(b).start()
         if b + 2 < blocks:
-            load(b + 2).start()
+            load(blocks + b + 2).start()
     store(blocks - 2).wait()
     store(blocks - 1).wait()
     for b in range(blocks):
@@ -982,15 +928,15 @@
     keep.wait()
 
 
-def run_ff(middle, dy, wff, normed_two_t, active, slope, gain, wout):
+def run_ff(middle, dy, wff, gain, offset, up_bias, wout):
     length, width = middle.shape
     half = wff.shape[3] // WIDE
     chunks = 2 * wff.shape[3] // CHUNK
-    blocks = length // BLOCK
+    blocks = length // PIECE
     pairs = wout.shape[0] // PAIR
     depth = width // SEQ_SIZE
     dma = pltpu.SemaphoreType.DMA
-    rows = pltpu.VMEM((blocks, BLOCK, width), BF)
+    rows = pltpu.VMEM((blocks, PIECE, width), BF)
     hidden = pltpu.VMEM((half, length, WIDE), BF)
     flat_t = pltpu.VMEM((width, length), BF)
     return pl.pallas_call(
@@ -1003,24 +949,24 @@
             shape_of((chunks, Z_SIZE, Y_SIZE, depth, CHUNK), BF),
             shape_of((SMALL_ROWS, width), F32),
         ],
-        in_specs=[ANY_SPEC] * 6 + [VMEM_SPEC, ANY_SPEC],
+        in_specs=[ANY_SPEC] * 3 + [VMEM_SPEC] * 3 + [ANY_SPEC],
         out_specs=[ANY_SPEC] * 5 + [VMEM_SPEC],
         scratch_shapes=[
             pltpu.VMEM((length, width), BF), pltpu.VMEM(wff.shape, BF),
-            pltpu.VMEM(wout.shape, BF),
+            pltpu.VMEM(wout.shape, BF), pltpu.VMEM((1, half * WIDE), F32),
             pltpu.VMEM((length, width), BF), flat_t, pltpu.VMEM((pairs, length, PAIR), BF),
-            flat_t, flat_t, hidden, hidden,
-            pltpu.VMEM((BLOCK, width), F32), rows, rows,
+            pltpu.VMEM((PIECE, width), BF), flat_t, flat_t, hidden, hidden,
+            pltpu.VMEM((PIECE, width), F32), rows, rows,
             pltpu.VMEM((chunks, Z_SIZE, Y_SIZE, CORES, depth, CHUNK), BF),
             pltpu.VMEM((chunks, Z_SIZE, Y_SIZE, depth, CHUNK), BF),
-            pltpu.VMEM((2, BLOCK, width), F32), pltpu.VMEM((2, BLOCK, width), F32),
+            pltpu.VMEM((2, PIECE, width), F32), pltpu.VMEM((2, PIECE, width), F32),
             dma((blocks,)), dma((blocks,)), dma((chunks,)), dma((chunks,)),
-            dma((2,)), dma((2,)), dma((1,)), dma((4 + 3 * half,)), dma((1 + 2 * blocks,)),
+            dma((2,)), dma((2,)), dma((1,)), dma((2 + half,)), dma((1 + 2 * blocks,)),
         ],
         compiler_params=pltpu.CompilerParams(
             collective_id=1, has_side_effects=True, vmem_limit_bytes=VMEM_LIMIT
         ),
-    )(middle, dy, wff, normed_two_t, active, slope, gain, wout)
+    )(middle, dy, wff, gain, offset, up_bias, wout)
 
 
 def back_kernel(
@@ -1505,15 +1451,12 @@
     out_bias, ln2_gain, ln2_bias, up_weight, up_bias, down_weight, down_bias, cotangent,
 ):
     x, dy = tokens[0], cotangent[0]
-    (
-        queries, keys, values, mixture, middle, normed_t, wff, key_more, query_more,
-        normed_two_t, active, slope,
-    ) = run_fwd(
-        x, segment_ids, context_flags, ln1_gain, ln1_bias, qv_bias, out_bias, ln2_gain,
-        ln2_bias, up_bias, qkv_weight, out_weight, up_weight, down_weight.T,
+    queries, keys, values, mixture, middle, normed_t, wff, key_more, query_more = run_fwd(
+        x, segment_ids, context_flags, ln1_gain, ln1_bias, qv_bias, out_bias, qkv_weight,
+        out_weight, up_weight, down_weight.T,
     )
     branch, grad_middle, ga_t, grad_mixture, ff_part, small = run_ff(
-        middle, dy, wff, normed_two_t, active, slope, ln2_gain, out_weight
+        middle, dy, wff, ln2_gain, ln2_bias, up_bias, out_weight
     )
     (
         output, tokens_grad, qkv_grad, out_grad, up_grad, down_grad, gain_one, offset_one,

time: 227 us -> 227 us (level)
    pallas_call x1, Pallas kernels: 66.5 us -> 60.9 us  [run_fwd(): pl.pallas_call(fwd_kernel, out_shape=[shape_of(by_pair, BF)] * 4 + [shape...]
    pallas_call x1, Pallas kernels: 55.5 us -> 60.8 us  [run_ff(): pl.pallas_call(ff_kernel, out_shape=[shape_of((length, width), BF), shape...]
where the time goes in v1:
time: 227 us
  Pallas kernels  226 us (100%)
    pallas_call x1, Pallas kernels, run_back(): pl.pallas_call(back_kernel, out_shape=[shape_of((length, width), BF), sha...  99.9 us
    pallas_call x1, Pallas kernels, run_fwd(): pl.pallas_call(fwd_kernel, out_shape=[shape_of(by_pair, BF)] * 4 + [shape...  60.9 us
    pallas_call x1, Pallas kernels, run_ff(): pl.pallas_call(ff_kernel, out_shape=[shape_of((length, width), BF), shape...  60.8 us

profile of v1, /device:TPU:0, one launch (start us, length us, event | category | flops | bytes accessed | tf_op | source)
XLA Modules:
  0.0 226.9 jit_solution(12558474248482556323)
XLA Ops:
  0.6 60.9 %shard_map.263 = (bf16[4,1024,128]{2,1,0:T(8,128)(2,1)}, bf16[4,1024,128]{2,1,0:T(8,128)(2,1)}, bf16[4,1024,128]{2,1,0:T(8,128)(2,1)}, bf16[4,1024,128]{2,1,0:T(...) custom-call(bf16[1024,1024]{1,0:T(8,128)(2,1)} %bitcast.7, ...), custom_call_target="tpu_custom_call" | custom-call | tf_op jit(solution)/shard_map/pallas_call | solution.py:697
  61.6 60.8 %shard_map.264 = (bf16[1024,1024]{1,0:T(8,128)(2,1)}, f32[1024,1024]{1,0:T(8,128)}, bf16[1024,1024]{1,0:T(8,128)(2,1)}, bf16[4,1024,128]{2,1,0:T(8,128)(2,1)}, b...) custom-call(f32[1024,1024]{1,0:T(8,128)} %get-tuple-element.61.mid_hbm, bf16[1024,1024]{1,0:T(8,128)(2,1)} %bitcast.9, ...), custom_call_target="tpu_custom_call" | custom-call | tf_op jit(solution)/shard_map/pallas_call | solution.py:942
  122.4 99.9 %shard_map.265 = (bf16[1024,1024]{1,0:T(8,128)(2,1)}, bf16[1024,1024]{1,0:T(8,128)(2,1)}, f32[3,64,512]{2,1,0:T(8,128)}, f32[64,512]{1,0:T(8,128)}, f32[64,2048]...) custom-call(bf16[4,1024,128]{2,1,0:T(8,128)(2,1)} %get-tuple-element, ...), custom_call_target="tpu_custom_call" | custom-call | tf_op jit(solution)/shard_map/pallas_call | solution.py:1372
  222.4 4.4 %shard_map.266 = (bf16[1024,1024]{1,0:T(8,128)(2,1)}, bf16[1024,1024]{1,0:T(8,128)(2,1)}, f32[3,64,512]{2,1,0:T(8,128)}, f32[64,512]{1,0:T(8,128)}, f32[64,2048]...) custom-call(bf16[1024,1024]{1,0:T(8,128)(2,1)} %get-tuple-element.72, ...), custom_call_target="tpu_custom_call" | custom-call | tf_op jit(solution)/shard_map/pallas_call | solution.py:1437

commit v2 on v1

--- a/solution.py
+++ b/solution.py
@@ -725,8 +725,8 @@
 
 def ff_kernel(
     mid_hbm, dy_hbm, wff_hbm, gain, offset, up_bias, wout_hbm,
-    branch_out, gmid_hbm, ga_out, gm_out, summed, small_ref,
-    dy_ref, wff, wout, bias_row, branch_ref, ga_t, gm_ref, normed, normed_t, dy_t, active, before_grad, gnt_acc, gnt_own, gnt_x, whole, from_mate,
+    branch_out, branch_first, gmid_hbm, ga_out, gm_out, summed, small_ref,
+    branch_x,    dy_ref, wff, wout, bias_row, branch_ref, ga_t, gm_ref, normed, normed_t, dy_t, active, before_grad, gnt_acc, gnt_own, gnt_x, whole, from_mate,
     held, ready,
     xs, xr, cs, cr, ls, ws, ss, ins, outs,
 ):
@@ -866,6 +866,10 @@
         return 0
 
     lax.fori_loop(0, length // BLOCK, branch, 0)
+    first_rows = remote(
+        branch_ref.at[0:BLOCK, :], branch_x, xs.at[blocks], xr.at[blocks], across
+    )
+    first_rows.start()
     branch_keep = pltpu.make_async_copy(branch_ref, branch_out, outs.at[0])
     branch_keep.start()
     wout_load.wait()
@@ -924,8 +928,12 @@
     for b in range(blocks):
         ga_copy(b).wait()
         gm_copy(b).wait()
+    first_rows.wait()
+    first_keep = pltpu.make_async_copy(branch_x, branch_first, outs.at[1 + 2 * blocks])
+    first_keep.start()
     branch_keep.wait()
     keep.wait()
+    first_keep.wait()
 
 
 def run_ff(middle, dy, wff, gain, offset, up_bias, wout):
@@ -943,6 +951,7 @@
         ff_kernel,
         out_shape=[
             shape_of((length, width), BF),
+            shape_of((BLOCK, width), BF),
             shape_of((length, width), F32),
             shape_of((width, length), BF),
             shape_of((pairs, length, PAIR), BF),
@@ -950,8 +959,9 @@
             shape_of((SMALL_ROWS, width), F32),
         ],
         in_specs=[ANY_SPEC] * 3 + [VMEM_SPEC] * 3 + [ANY_SPEC],
-        out_specs=[ANY_SPEC] * 5 + [VMEM_SPEC],
+        out_specs=[ANY_SPEC] * 6 + [VMEM_SPEC],
         scratch_shapes=[
+            pltpu.VMEM((BLOCK, width), BF),
             pltpu.VMEM((length, width), BF), pltpu.VMEM(wff.shape, BF),
             pltpu.VMEM(wout.shape, BF), pltpu.VMEM((1, half * WIDE), F32),
             pltpu.VMEM((length, width), BF), flat_t, pltpu.VMEM((pairs, length, PAIR), BF),
@@ -960,8 +970,8 @@
             pltpu.VMEM((chunks, Z_SIZE, Y_SIZE, CORES, depth, CHUNK), BF),
             pltpu.VMEM((chunks, Z_SIZE, Y_SIZE, depth, CHUNK), BF),
             pltpu.VMEM((2, PIECE, width), F32), pltpu.VMEM((2, PIECE, width), F32),
-            dma((blocks,)), dma((blocks,)), dma((chunks,)), dma((chunks,)),
-            dma((2,)), dma((2,)), dma((1,)), dma((2 + half,)), dma((1 + 2 * blocks,)),
+            dma((blocks + 1,)), dma((blocks + 1,)), dma((chunks,)), dma((chunks,)),
+            dma((2,)), dma((2,)), dma((1,)), dma((2 + half,)), dma((2 + 2 * blocks,)),
         ],
         compiler_params=pltpu.CompilerParams(
             collective_id=1, has_side_effects=True, vmem_limit_bytes=VMEM_LIMIT
@@ -971,7 +981,7 @@
 
 def back_kernel(
     q_hbm, k_hbm, v_hbm, mix_hbm, gm_hbm, query_hbm, ga_hbm, normed_hbm, wqkv_hbm, x_hbm,
-    key_more, gain, down_bias, small_in, mid_hbm, gmid_hbm, ff_part, branch,
+    key_more, gain, down_bias, small_in, mid_hbm, gmid_hbm, ff_part, branch, branch_first,
     out_hbm, tokens_hbm, qkv_sum, out_sum, up_sum, down_sum,
     gain_one, offset_one, qv_small, out_small, gain_two, offset_two, up_small, down_small,
     q_ref, k_ref, v_ref, mix_ref, gm_ref, query_more, ga_t, normed_t, wqkv, x_ref,
@@ -1023,6 +1033,8 @@
     def part(b):
         return pl.ds(b * BLOCK, BLOCK)
 
+    first_load = pltpu.make_async_copy(branch_first, branch_x.at[part(0), :], br.at[0])
+
     def branch_copy(b):
         return remote(branch.at[part(b), :], branch_x.at[part(b), :], bs.at[b], br.at[b], across)
 
@@ -1126,7 +1138,10 @@
         )
 
     def branch_event(b):
-        branch_copy(b).wait_recv()
+        if b == 0:
+            first_load.wait()
+        else:
+            branch_copy(b).wait_recv()
         load(b).wait()
         branch_load(b).wait()
         both = branch_own[b % 2].astype(F32) + branch_x[part(b), :].astype(F32)
@@ -1136,7 +1151,8 @@
         if b + 2 < blocks:
             branch_load(b + 2).start()
 
-    for b in range(blocks):
+    first_load.start()
+    for b in range(1, blocks):
         branch_copy(b).start()
     for n in range(2):
         load(n).start()
@@ -1182,14 +1198,15 @@
         query_side = jnp.concatenate([queries, more], axis=1)
         grad_side = jnp.concatenate([grads, in_pieces(inner, 0, 0.0)], axis=1)
         to_queries = jnp.zeros((PAIR, 2 * STRIP), F32)
-        for n in range(blocks):
-            keys = jnp.concatenate([k_ref[p, part(n), :], key_more[part(n), :]], axis=1)
-            values = jnp.concatenate([v_ref[p, part(n), :], one_lanes(BLOCK)], axis=1)
+        for n in range(strips):
+            cut = pl.ds(n * STRIP, STRIP)
+            keys = jnp.concatenate([k_ref[p, cut, :], key_more[cut, :]], axis=1)
+            values = jnp.concatenate([v_ref[p, cut, :], one_lanes(STRIP)], axis=1)
             weights = jnp.exp(dot_rows(keys, query_side)).astype(BF)
             grad_scores = weights * dot_rows(values, grad_side).astype(BF)
-            value_acc[part(n), :] += split_sum(weights, grads)
-            key_acc[part(n), :] += split_sum(grad_scores, queries)
-            to_queries += nn(key_t[:, part(n)], grad_scores)
+            value_acc[cut, :] += split_sum(weights, grads)
+            key_acc[cut, :] += split_sum(grad_scores, queries)
+            to_queries += nn(key_t[:, cut], grad_scores)
         own = jnp.concatenate(
             [to_queries[:HEAD_DIM, :STRIP], to_queries[HEAD_DIM:, STRIP:]], axis=0
         )
@@ -1339,7 +1356,8 @@
     for b in range(blocks):
         out_copy(b).wait()
         tokens_copy(b).wait()
-        branch_copy(b).wait_send()
+        if b > 0:
+            branch_copy(b).wait_send()
     for g in range(groups):
         ff_y_copy(g).wait_send()
         for d in (1, 2, 3):
@@ -1354,6 +1372,7 @@
 def run_back(
     queries, keys, values, mixture, grad_mixture, query_more, ga_t, normed_t, wqkv, x,
     key_more, gain, down_bias, small, middle, grad_middle, ff_part, branch,
+    branch_first,
 ):
     length, width = x.shape
     pairs = queries.shape[0]
@@ -1380,7 +1399,7 @@
             shape_of((depth, hidden), F32),
             row, row, shape_of((2, cols), F32), row, row, row, shape_of((hidden,), F32), row,
         ],
-        in_specs=[ANY_SPEC] * 10 + [VMEM_SPEC] * 4 + [ANY_SPEC] * 4,
+        in_specs=[ANY_SPEC] * 10 + [VMEM_SPEC] * 4 + [ANY_SPEC] * 5,
         out_specs=[ANY_SPEC] * 2 + [VMEM_SPEC] * 12,
         scratch_shapes=[pltpu.VMEM(v.shape, BF) for v in loaded] + [
             whole_rows, whole_rows, pltpu.VMEM((PAIR, length), BF),
@@ -1410,7 +1429,10 @@
         compiler_params=pltpu.CompilerParams(
             collective_id=2, has_side_effects=True, vmem_limit_bytes=VMEM_LIMIT
         ),
-    )(*loaded, key_more, gain, down_bias, small, middle, grad_middle, ff_part, branch)
+    )(
+        *loaded, key_more, gain, down_bias, small, middle, grad_middle, ff_part, branch,
+        branch_first,
+    )
 
 
 def hand_over_kernel(*refs):
@@ -1455,7 +1477,7 @@
         x, segment_ids, context_flags, ln1_gain, ln1_bias, qv_bias, out_bias, qkv_weight,
         out_weight, up_weight, down_weight.T,
     )
-    branch, grad_middle, ga_t, grad_mixture, ff_part, small = run_ff(
+    branch, branch_first, grad_middle, ga_t, grad_mixture, ff_part, small = run_ff(
         middle, dy, wff, ln2_gain, ln2_bias, up_bias, out_weight
     )
     (
@@ -1464,6 +1486,7 @@
     ) = hand_over(run_back(
         queries, keys, values, mixture, grad_mixture, query_more, ga_t, normed_t, qkv_weight, x,
         key_more, ln1_gain, down_bias, small, middle, grad_middle, ff_part, branch,
+        branch_first,
     ))
     return (
         output[None], tokens_grad[None], gain_one, offset_one, qkv_grad, qv_grad, out_grad.T,

time: 227 us -> 233 us (1.026)
  Pallas kernels: 226 us -> 232 us
    pallas_call x1, Pallas kernels: 60.8 us -> 68.5 us  [run_ff(): pl.pallas_call(ff_kernel, out_shape=[shape_of((length, width), BF), shape...]
where the time goes in v2:
time: 233 us; the launch traced here: 232 us
  Pallas kernels  232 us (100%)
    pallas_call x1, Pallas kernels, run_back(): pl.pallas_call(back_kernel, out_shape=[shape_of((length, width), BF), sha...  97.8 us
    pallas_call x1, Pallas kernels, run_ff(): pl.pallas_call(ff_kernel, out_shape=[shape_of((length, width), BF), shape...  68.5 us
    pallas_call x1, Pallas kernels, run_fwd(): pl.pallas_call(fwd_kernel, out_shape=[shape_of(by_pair, BF)] * 4 + [shape...  60.9 us

profile of v2, /device:TPU:0, one launch (start us, length us, event | category | flops | bytes accessed | tf_op | source)
XLA Modules:
  0.0 232.5 jit_solution(5285600529771792012)
XLA Ops:
  0.6 60.9 %shard_map.263 = (bf16[4,1024,128]{2,1,0:T(8,128)(2,1)}, bf16[4,1024,128]{2,1,0:T(8,128)(2,1)}, bf16[4,1024,128]{2,1,0:T(8,128)(2,1)}, bf16[4,1024,128]{2,1,0:T(...) custom-call(bf16[1024,1024]{1,0:T(8,128)(2,1)} %bitcast.7, ...), custom_call_target="tpu_custom_call" | custom-call | tf_op jit(solution)/shard_map/pallas_call | solution.py:697
  61.6 68.5 %shard_map.264 = (bf16[1024,1024]{1,0:T(8,128)(2,1)}, bf16[256,1024]{1,0:T(8,128)(2,1)}, f32[1024,1024]{1,0:T(8,128)}, bf16[1024,1024]{1,0:T(8,128)(2,1)}, bf16[...) custom-call(f32[1024,1024]{1,0:T(8,128)} %get-tuple-element.62.mid_hbm, ...), custom_call_target="tpu_custom_call" | custom-call | tf_op jit(solution)/shard_map/pallas_call | solution.py:950
  130.1 97.8 %shard_map.265 = (bf16[1024,1024]{1,0:T(8,128)(2,1)}, bf16[1024,1024]{1,0:T(8,128)(2,1)}, f32[3,64,512]{2,1,0:T(8,128)}, f32[64,512]{1,0:T(8,128)}, f32[64,2048]...) custom-call(bf16[4,1024,128]{2,1,0:T(8,128)(2,1)} %get-tuple-element, ...), custom_call_target="tpu_custom_call" | custom-call | tf_op jit(solution)/shard_map/pallas_call | solution.py:1391
  227.9 4.4 %shard_map.266 = (bf16[1024,1024]{1,0:T(8,128)(2,1)}, bf16[1024,1024]{1,0:T(8,128)(2,1)}, f32[3,64,512]{2,1,0:T(8,128)}, f32[64,512]{1,0:T(8,128)}, f32[64,2048]...) custom-call(bf16[1024,1024]{1,0:T(8,128)(2,1)} %get-tuple-element.74, ...), custom_call_target="tpu_custom_call" | custom-call | tf_op jit(solution)/shard_map/pallas_call | solution.py:1459
